TPU v7x, 256 devices: a whole 4x4x8 slice. The times are simulated.
256 devices in a mesh: tea: 8 (over z), stu: 16 (over y, x), hid: 2 (over core).
Axes of the slice: x: 4, y: 4, z: 8, core: 2. Of those that a mesh axis runs over, the one named last changes fastest.
Arguments:
- teacher_hidden: bfloat16 [16384, 8192], P('tea', 'hid'), may hold values from -60 to 60
- projection: bfloat16 [4096, 8192], P('stu', 'hid'), may hold values from -7 to 7
- student_hidden: bfloat16 [10240, 4096], P('stu'), may hold values from -600 to 600
- teacher_segment: int32 [16384], P(('tea', 'hid')), may hold values from 0 to 15, never falling along the last dimension, each value on 1 to 2048 neighbouring positions
- student_segment: int32 [10240], P('stu'), may hold values from 0 to 15, never falling along the last dimension, each value on 1 to 1280 neighbouring positions
Outputs:
- plan: bfloat16 [16384, 10240], P(('tea', 'hid'), 'stu')
- row_pot: float32 [16384], P(('tea', 'hid'))
- col_pot: float32 [10240], P('stu')
Inputs may be any that keep to these rules, and one draw needn't show every extreme that they name: `teacher_segment`: never falls along the tokens, and every number of 0 to 15 appears. `student_segment`: never falls along the tokens, and every number of 0 to 15 appears.
All inputs are finite; a program needn't handle non-finite values.
Results may differ from a plain program's by a relative error of at most 0.0073.
Values may be sent and summed in bfloat16 or wider, within the bound.
A program may use at most 192 MiB of HBM per device.

v0:
```python
import jax
import jax.numpy as jnp
from jax import lax
from jax.sharding import PartitionSpec as P

ITERS = 3


EPSILON = 0.004
FLOOR = -1e30
CONTRACT_FIRST = (((0,), (1,)), ((), ()))
CONTRACT_LAST = (((1,), (1,)), ((), ()))


def shifted_sum(values, support, top, axis):
    spread = jnp.expand_dims(top, axis)
    terms = jnp.where(support, jnp.exp(jnp.where(support, values, spread) - spread), 0.0)
    return jnp.sum(terms, axis=axis)


def row_lse(values, support):
    top = jnp.max(jnp.where(support, values, FLOOR), axis=1)
    top = lax.pmax(top, "stu")
    total = lax.psum(shifted_sum(values, support, top, 1), "stu")
    return top + jnp.log(total)


def col_lse(values, support):
    top = jnp.max(jnp.where(support, values, FLOOR), axis=0)
    top = lax.pmax(top, ("tea", "hid"))
    total = lax.psum(shifted_sum(values, support, top, 0), ("tea", "hid"))
    return top + jnp.log(total)


def per_device(teacher_hidden, projection, student_hidden, teacher_segment, student_segment):
    partial_proj = lax.dot_general(
        projection, teacher_hidden, CONTRACT_LAST, preferred_element_type=jnp.float32
    )
    projected = lax.psum_scatter(partial_proj, "hid", scatter_dimension=1, tiled=True).astype(
        jnp.bfloat16
    )
    own_rows = projected.shape[1]
    own_cols = student_hidden.shape[0]
    student_inv = lax.rsqrt(
        jnp.einsum("cd,cd->c", student_hidden, student_hidden, preferred_element_type=jnp.float32)
        + 1e-06
    )
    piece = lax.all_gather(projected, "stu", axis=0, tiled=True)
    dots = lax.dot_general(
        piece, student_hidden, CONTRACT_FIRST, preferred_element_type=jnp.float32
    )
    squares = jnp.einsum("fr,fr->r", piece, piece, preferred_element_type=jnp.float32)
    dots, squares = (dots, squares)
    teacher_inv = lax.rsqrt(squares + 1e-06)
    scaled = (dots * teacher_inv[:, None] * student_inv[None, :] - 1.0) / EPSILON
    support = teacher_segment[:, None] == student_segment[None, :]
    row_log = jnp.log(lax.psum(jnp.sum(support, axis=1).astype(jnp.float32), "stu"))
    col_log = jnp.log(lax.psum(jnp.sum(support, axis=0).astype(jnp.float32), ("tea", "hid")))
    row_pot = jnp.zeros((own_rows,), jnp.float32)
    col_pot = jnp.zeros((own_cols,), jnp.float32)
    for step in range(ITERS):
        row_pot = row_log - row_lse(scaled + col_pot[None, :], support)
        col_pot = col_log - col_lse(scaled + row_pot[:, None], support)
    plan = jnp.where(support, jnp.exp(scaled + row_pot[:, None] + col_pot[None, :]), 0.0)
    return (plan.astype(jnp.bfloat16), row_pot, col_pot)


def solution(mesh):
    placed = (P("tea", "hid"), P("stu", "hid"), P("stu", None), P(("tea", "hid")), P("stu"))
    return jax.shard_map(
        per_device,
        mesh=mesh,
        in_specs=placed,
        out_specs=(P(("tea", "hid"), "stu"), P(("tea", "hid")), P("stu")),
        check_vma=False,
    )
```

profile of v0, /device:TPU:1, one launch (start us, length us, event | category | flops | bytes accessed | tf_op | source)
XLA Modules:
  0.0 532.7 jit_solution(4033122979855495577)
XLA Ops:
  7.2 0.0 copy-start
  7.2 0.0 reduce-scatter.2.cloned.1.call-start
  7.2 1.5 copy-done
  8.8 9.5 %fusion.29 = f32[256,2048]{1,0:T(8,128)} fusion(bf16[256,4096]{1,0:T(8,128)(2,1)S(1)} %copy-done, bf16[2048,4096]{1,0:T(8,128)(2,1)} %param.5), kind=kOutput, calls=%fused_computation.60 | convolution fusion | flops 4294967296 | bytes 20971520 | tf_op jit(solution)/shard_map/dot_general | solution.py:36
  18.2 0.0 copy-start.2
  18.2 0.0 copy-start.3
  18.3 0.0 reduce-scatter.2.cloned.1.call-update
  18.3 0.2 all-gather.2.cloned.1.call-start
  18.5 19.3 %reduce-scatter.2.cloned.1.call-done = f32[256,1024]{1,0:T(8,128)} async-done(((f32[256,2048]{1,0:T(8,128)}), f32[256,1024]{1,0:T(8,128)}) %reduce-scatter.2.cloned.1.call-update) | async-done | bytes 1048592 | tf_op jit(solution)/shard_map/reduce_scatter | solution.py:39
  37.8 2.1 convert_element_type.16
  39.9 0.0 all-gather.2.cloned.1.call-update
  39.9 0.0 copy-done.2
  39.9 0.0 copy-done.3
  39.9 0.5 fusion.2
  40.4 3.6 fusion.1
  44.0 73.5 %all-gather.2.cloned.1.call-done = bf16[4096,1024]{1,0:T(8,128)(2,1)} async-done(((bf16[256,1024]{1,0:T(8,128)(2,1)}), bf16[4096,1024]{1,0:T(8,128)(2,1)}) %all-gather.2.cloned.1.call-update) | async-done | bytes 8388624 | tf_op jit(solution)/shard_map/all_gather | solution.py:48
  117.6 0.0 copy-start.1
  117.6 5.2 fusion
  122.8 0.5 copy-done.1
  123.3 11.4 %fusion.4 = (f32[1024]{0:T(1024)S(1)}, f32[1024,640]{1,0:T(8,128)}) fusion(s32[640]{0:T(1024)S(1)} %copy-done.2, s32[1024]{0:T(1024)S(1)} %copy-done.3, f32[640]{0:T(1024)S(1)} %add_rsqrt_fusion, f32[1024]{0:T(1024)S(1)} %add_rsqrt_fusion.1, bf16[4096,1024]{1,0:T(8,128)(2,1)S(1)} %copy-done.1, bf16[640,4096]{1,0:T(8,128)(2,1)} %param.7), kind=kOutput, calls=%fused_computation.26 | convolution fusion | flops 5373295616 | bytes 16270336 | tf_op jit(solution)/shard_map/dot_general | solution.py:49
  134.7 31.4 %pmax.42 = f32[1024]{0:T(1024)S(1)} all-reduce(f32[1024]{0:T(1024)S(1)} %get-tuple-element.9), channel_id=1, replica_groups=mesh['tea'=8,'stu'=16,'hid'=2] {'stu'}, use_global_device_ids=true, to_apply=%region_6.7 | all-reduce | flops 1024 | bytes 8192 | tf_op jit(solution)/shard_map/pmax | solution.py:23
  166.1 2.5 fusion.7
  168.6 29.0 %all-reduce.1 = (f32[1024]{0:T(1024)S(1)}, f32[1024]{0:T(1024)S(1)}) all-reduce(f32[1024]{0:T(1024)S(1)} %fusion.7, f32[1024]{0:T(1024)S(1)} %convert_element_type.18), channel_id=1, replica_groups=mesh['tea'=8,'stu'=16,'hid'=2] {'stu'}, use_global_device_ids=true, to_apply=%region_8.9 | all-reduce | flops 2048 | bytes 16384 | tf_op jit(solution)/shard_map/psum | solution.py:24
  197.7 2.2 fusion.8
  199.8 38.2 %pmax.43 = f32[640]{0:T(1024)S(1)} all-reduce(f32[640]{0:T(1024)S(1)} %fusion.8), channel_id=1, replica_groups=mesh['tea'=8,'stu'=16,'hid'=2] {'tea','hid'}, use_global_device_ids=true, to_apply=%region_10.11 | all-reduce | flops 640 | bytes 5120 | tf_op jit(solution)/shard_map/pmax | solution.py:30
  238.1 2.2 fusion.11
  240.3 23.5 %all-reduce = (f32[640]{0:T(1024)S(1)}, f32[640]{0:T(1024)S(1)}) all-reduce(f32[640]{0:T(1024)S(1)} %fusion.11, f32[640]{0:T(1024)S(1)} %convert_element_type.19), channel_id=1, replica_groups=mesh['tea'=8,'stu'=16,'hid'=2] {'tea','hid'}, use_global_device_ids=true, to_apply=%region_12.13 | all-reduce | flops 1280 | bytes 10240 | tf_op jit(solution)/shard_map/psum | solution.py:31
  263.8 2.2 fusion.12
  266.1 30.2 %pmax.44 = f32[1024]{0:T(1024)S(1)} all-reduce(f32[1024]{0:T(1024)S(1)} %fusion.12), channel_id=1, replica_groups=mesh['tea'=8,'stu'=16,'hid'=2] {'stu'}, use_global_device_ids=true, to_apply=%region_14.15 | all-reduce | flops 1024 | bytes 8192 | tf_op jit(solution)/shard_map/pmax | solution.py:23
  296.3 2.4 fusion.15
  298.7 28.5 %psum.60 = f32[1024]{0:T(1024)S(1)} all-reduce(f32[1024]{0:T(1024)S(1)} %fusion.15), channel_id=1, replica_groups=mesh['tea'=8,'stu'=16,'hid'=2] {'stu'}, use_global_device_ids=true, to_apply=%region_16.17 | all-reduce | flops 1024 | bytes 8192 | tf_op jit(solution)/shard_map/psum | solution.py:24
  327.2 2.2 fusion.16
  329.4 38.1 %pmax.45 = f32[640]{0:T(1024)S(1)} all-reduce(f32[640]{0:T(1024)S(1)} %fusion.16), channel_id=1, replica_groups=mesh['tea'=8,'stu'=16,'hid'=2] {'tea','hid'}, use_global_device_ids=true, to_apply=%region_18.19 | all-reduce | flops 640 | bytes 5120 | tf_op jit(solution)/shard_map/pmax | solution.py:30
  367.5 2.2 fusion.19
  369.7 23.6 %psum.61 = f32[640]{0:T(1024)S(1)} all-reduce(f32[640]{0:T(1024)S(1)} %fusion.19), channel_id=1, replica_groups=mesh['tea'=8,'stu'=16,'hid'=2] {'tea','hid'}, use_global_device_ids=true, to_apply=%region_20.21 | all-reduce | flops 640 | bytes 5120 | tf_op jit(solution)/shard_map/psum | solution.py:31
  393.3 2.2 fusion.20
  395.5 30.2 %pmax.46 = f32[1024]{0:T(1024)S(1)} all-reduce(f32[1024]{0:T(1024)S(1)} %fusion.20), channel_id=1, replica_groups=mesh['tea'=8,'stu'=16,'hid'=2] {'stu'}, use_global_device_ids=true, to_apply=%region_22.23 | all-reduce | flops 1024 | bytes 8192 | tf_op jit(solution)/shard_map/pmax | solution.py:23
  425.8 2.4 fusion.23
  428.2 28.5 %psum.62 = f32[1024]{0:T(1024)S(1)} all-reduce(f32[1024]{0:T(1024)S(1)} %fusion.23), channel_id=1, replica_groups=mesh['tea'=8,'stu'=16,'hid'=2] {'stu'}, use_global_device_ids=true, to_apply=%region_24.25 | all-reduce | flops 1024 | bytes 8192 | tf_op jit(solution)/shard_map/psum | solution.py:24
  456.7 0.0 copy-start.4
  456.7 2.2 fusion.24
  458.9 37.7 %pmax.47 = f32[640]{0:T(1024)S(1)} all-reduce(f32[640]{0:T(1024)S(1)} %fusion.24), channel_id=1, replica_groups=mesh['tea'=8,'stu'=16,'hid'=2] {'tea','hid'}, use_global_device_ids=true, to_apply=%region_26.27 | all-reduce | flops 640 | bytes 5120 | tf_op jit(solution)/shard_map/pmax | solution.py:30
  496.6 2.2 fusion.27
  498.8 23.6 %psum.63 = f32[640]{0:T(1024)S(1)} all-reduce(f32[640]{0:T(1024)S(1)} %fusion.27), channel_id=1, replica_groups=mesh['tea'=8,'stu'=16,'hid'=2] {'tea','hid'}, use_global_device_ids=true, to_apply=%region_28.29 | all-reduce | flops 640 | bytes 5120 | tf_op jit(solution)/shard_map/psum | solution.py:31
  522.4 0.0 copy-done.4
  522.4 0.0 copy-start.5
  522.4 3.4 fusion.28
  525.8 0.0 copy-done.5
  (10 shorter events, 0.1 us)
Async XLA Ops:
  7.2 1.6 copy-start
  7.2 30.6 %reduce-scatter.2.cloned.1.call-start = ((), (), s32[]{:S(2)}) async-start(), calls=%async_computation.1 | async-start | bytes 3145728 | tf_op jit(solution)/shard_map/reduce_scatter | solution.py:39
  18.2 21.6 %copy-start.2 = (s32[640]{0:T(1024)S(1)}, s32[640]{0:T(1024)}, u32[]{:S(2)}) copy-start(s32[640]{0:T(1024)} %param.9) | copy-start | bytes 7684
  18.2 21.6 %copy-start.3 = (s32[1024]{0:T(1024)S(1)}, s32[1024]{0:T(1024)}, u32[]{:S(2)}) copy-start(s32[1024]{0:T(1024)} %param.8) | copy-start | bytes 12292
  18.3 99.3 %all-gather.2.cloned.1.call-start = ((), (), s32[]{:S(2)}) async-start(), calls=%async_computation.2 | async-start | bytes 8912896 | tf_op jit(solution)/shard_map/all_gather | solution.py:48
  117.6 5.8 %copy-start.1 = (bf16[4096,1024]{1,0:T(8,128)(2,1)S(1)}, bf16[4096,1024]{1,0:T(8,128)(2,1)}, u32[]{:S(2)}) copy-start(bf16[4096,1024]{1,0:T(8,128)(2,1)} %all-gather.2.cloned.1.call-done) | copy-start | bytes 25165828
  456.7 65.7 %copy-start.4 = (f32[1024]{0:T(1024)}, f32[1024]{0:T(1024)S(1)}, u32[]{:S(2)}) copy-start(f32[1024]{0:T(1024)S(1)} %add_subtract_fusion.1) | copy-start | bytes 12292
  522.4 3.4 copy-start.5
Sparse Core Ops, SparseCore 0:
  18.4 19.3 reduce-scatter.1
  41.1 76.4 all-gather.1
where the time goes:
time: 534 us; the launch traced here: 533 us
  blocking collectives  363 us (68%)
  waiting for transfers between devices  92.8 us (17%)
  other arithmetic  39.8 us (7%)
  matrix products  20.9 us (4%)
  between operations  14.2 us (3%)
    pmax x3, blocking collectives, col_lse(): top = lax.pmax(top, ('tea', 'hid'))  114 us
    pmax x3, blocking collectives, row_lse(): top = lax.pmax(top, 'stu')  91.8 us
    psum x3, blocking collectives, row_lse(): total = lax.psum(shifted_sum(values, support, top, 1), 'stu')  86 us
    all_gather x1, waiting for transfers between devices, per_device(): piece = lax.all_gather(projected, 'stu', axis=0, tiled=True)  73.5 us
    psum x3, blocking collectives, col_lse(): total = lax.psum(shifted_sum(values, support, top, 0), ('tea', 'hid'))  70.6 us
    reduce_scatter x1, waiting for transfers between devices, per_device(): lax.psum_scatter(partial_proj, 'hid', scatter_dimension=1, tiled=True)  19.3 us
    reduce_sum x6, other arithmetic, shifted_sum(): return jnp.sum(terms, axis=axis)  13.9 us
    dot_general x1, matrix products, per_device(): lax.dot_general(piece, student_hidden, CONTRACT_FIRST, preferred_element_...  11.4 us
  transfers between devices with their start and end apart: 2, of which 2 were waited for; matrix products, arithmetic and copies ran while one was open for 1% of the time, Pallas kernels for 0%

commit v1 on v0

v1 whole, which is shorter than its diff:
```python
import functools

import jax
import jax.numpy as jnp
import numpy as np
from jax import lax
from jax.experimental import pallas as pl
from jax.experimental.pallas import tpu as pltpu
from jax.sharding import PartitionSpec as P

ITERS = 3
INV_EPSILON = float(np.float32(1.0) / np.float32(0.004))
FLOOR = -1e30
SAFE = -1e29
LANES = 128
ROW_BLOCK = 128
CHUNKS = 4
RING = 4
CONTRACT_LAST = (((1,), (1,)), ((), ()))


def to_lanes(part, combine):
    return combine(jnp.transpose(part), axis=0, keepdims=True)


def to_rows(vector):
    count = vector.shape[1]
    return jnp.transpose(jnp.broadcast_to(vector, (LANES, count)))


def merge(slots, width):
    tops, sums, counts = (slots[:, :, k * width:(k + 1) * width] for k in range(3))
    top = jnp.max(tops, axis=0)
    total = jnp.sum(sums * jnp.exp(tops - top), axis=0)
    return top, total, jnp.sum(counts, axis=0)


def kernel(
    peers,
    teacher_ref, proj_ref, student_ref, tseg_ref, sseg_ref,
    plan_ref, row_out, col_out,
    teacher, proj, student, theirs, mine, incoming, gathered, squares, highest, sinv,
    scaled, left, right, spare, row_first, row_next, col_first, col_next,
    teacher_sem, weight_sem, core_send, core_recv, ring_send, ring_recv, send_sem, recv_sem,
):
    rows, cols = scaled.shape
    feats = proj.shape[0]
    chunk = rows // CHUNKS
    half = chunk // 2
    blocks = rows // ROW_BLOCK
    strips = [slice(k * LANES, (k + 1) * LANES) for k in range(cols // LANES)]
    cores = 2
    stu = lax.axis_index("stu")
    hid = lax.axis_index("hid")
    place = lax.axis_index("tea") * cores + hid

    y, x = stu // RING, lax.rem(stu, RING)
    major, minor = y + hid * (x - y), x + hid * (y - x)

    def stu_of(big, small):
        return (big + hid * (small - big)) * RING + small + hid * (big - small)

    def around(index, step):
        return lax.rem(index + step + RING, RING)

    def stu_peer(step):
        return {"stu": lax.rem(stu + step, peers)}

    def tea_peer(step):
        other = lax.rem(place + step, peers)
        return {"tea": other // cores, "hid": lax.rem(other, cores)}

    def teacher_copy(c, whose):
        start = pl.multiple_of((whose * CHUNKS + c) * chunk, chunk)
        return pltpu.make_async_copy(
            teacher_ref.at[pl.ds(start, chunk)], teacher.at[whose * CHUNKS + c], teacher_sem.at[whose * CHUNKS + c]
        )

    proj_copy = pltpu.make_async_copy(proj_ref, proj, weight_sem.at[0])
    proj_copy.start()

    @pl.loop(0, CHUNKS)
    def _(c):
        teacher_copy(c, 1 - hid).start()
        teacher_copy(c, hid).start()

    @pl.loop(0, peers)
    def _(slot):
        big, small = slot // RING, lax.rem(slot, RING)
        source = pl.multiple_of(stu_of(big, small) * feats, feats)
        target = pl.multiple_of(small * feats, feats)
        pltpu.make_async_copy(
            student_ref.at[:, pl.ds(source, feats)], student.at[big, :, pl.ds(target, feats)], weight_sem.at[1]
        ).start()

    barrier = pltpu.get_barrier_semaphore()

    @pl.loop(1, peers)
    def _(step):
        pl.semaphore_signal(barrier, inc=1, device_id=stu_peer(step))
        pl.semaphore_signal(barrier, inc=1, device_id=tea_peer(step))

    left[...] = to_rows(tseg_ref[...].astype(jnp.float32))
    proj_copy.wait()
    pl.semaphore_wait(barrier, 2 * (peers - 1))

    def project(c, whose):
        teacher_copy(c, whose).wait()
        return lax.dot_general(
            teacher[whose * CHUNKS + c], proj[...], CONTRACT_LAST, preferred_element_type=jnp.float32
        )

    def core_copy(c):
        return pltpu.make_async_remote_copy(
            src_ref=theirs.at[c], dst_ref=incoming.at[c],
            send_sem=core_send.at[c], recv_sem=core_recv.at[c], device_id={"hid": 1 - hid},
        )

    def ring_copy(c, stage, ref, big, small):
        return pltpu.make_async_remote_copy(
            src_ref=ref, dst_ref=ref,
            send_sem=ring_send.at[c, stage], recv_sem=ring_recv.at[c, stage],
            device_id={"stu": stu_of(around(big, 0), around(small, 0))},
        )

    def block(c, small, part=slice(None)):
        return gathered.at[c, major, part, pl.ds(pl.multiple_of(around(small, 0) * feats, feats), feats)]

    def bundle(c, big, part=slice(None)):
        return gathered.at[c, around(big, 0), part]

    low, high = pl.ds(0, half), pl.ds(half, half)

    def sends(c, k):
        return [
            lambda: ring_copy(c, 0, block(c, minor), major, minor + 1),
            lambda: ring_copy(c, 1, block(c, minor), major, minor - 1),
            lambda: ring_copy(c, 2, block(c, minor - 1, low), major, minor + 1),
            lambda: ring_copy(c, 3, block(c, minor + 1, high), major, minor - 1),
            lambda: ring_copy(c, 4, bundle(c, major), major + 1, minor),
            lambda: ring_copy(c, 5, bundle(c, major), major - 1, minor),
            lambda: ring_copy(c, 6, bundle(c, major - 1, low), major + 1, minor),
            lambda: ring_copy(c, 7, bundle(c, major + 1, high), major - 1, minor),
        ][k]()

    def arrives(c, k):
        return [
            lambda: ring_copy(c, 0, block(c, minor - 1), major, minor + 1),
            lambda: ring_copy(c, 1, block(c, minor + 1), major, minor - 1),
            lambda: ring_copy(c, 2, block(c, minor + 2, low), major, minor + 1),
            lambda: ring_copy(c, 3, block(c, minor + 2, high), major, minor - 1),
            lambda: ring_copy(c, 4, bundle(c, major - 1), major + 1, minor),
            lambda: ring_copy(c, 5, bundle(c, major + 1), major - 1, minor),
            lambda: ring_copy(c, 6, bundle(c, major + 2, low), major + 1, minor),
            lambda: ring_copy(c, 7, bundle(c, major + 2, high), major - 1, minor),
        ][k]()

    def by_block(body, init=None, first=0, count=blocks):
        def step(b, carry):
            return body(pl.ds(pl.multiple_of(b * ROW_BLOCK, ROW_BLOCK), ROW_BLOCK), carry)
        return lax.fori_loop(first, first + count, step, init)

    def student_norms():
        pltpu.make_async_copy(student, student, weight_sem.at[1]).wait()

        @pl.loop(0, cols // LANES)
        def _(k):
            at = pl.ds(pl.multiple_of(k * LANES, LANES), LANES)
            def add(big, total):
                for j in range(RING * feats // LANES):
                    value = student[big, at, j * LANES:(j + 1) * LANES].astype(jnp.float32)
                    total += value * value
                return total
            total = lax.fori_loop(0, RING, add, jnp.zeros((LANES, LANES), jnp.float32))
            sinv[:, at] = lax.rsqrt(to_lanes(total, jnp.sum) + 1e-06)

    def first_rows(at, carry):
        tinv = lax.rsqrt(jnp.sum(squares[at, :], axis=1, keepdims=True) + 1e-06)
        tseg = left[at, :]
        tops = jnp.full((ROW_BLOCK, LANES), SAFE, jnp.float32)
        count = jnp.zeros((ROW_BLOCK, LANES), jnp.float32)
        for strip in strips:
            support = tseg == sseg_ref[:, strip].astype(jnp.float32)
            value = (scaled[at, strip] * tinv * sinv[:, strip] - 1.0) * INV_EPSILON
            value = jnp.where(support, value, FLOOR)
            scaled[at, strip] = value
            tops = jnp.maximum(tops, value)
            count += jnp.where(support, 1.0, 0.0)
        top = jnp.max(tops, axis=1, keepdims=True)
        total = jnp.zeros((ROW_BLOCK, LANES), jnp.float32)
        for strip in strips:
            total += jnp.exp(scaled[at, strip] - top)
        highest[at, :] = jnp.broadcast_to(top, (ROW_BLOCK, LANES))
        right[at, :] = total
        spare[at, :] = count
        return carry

    def multiply(c):
        at = pl.ds(pl.multiple_of(c * chunk, chunk), chunk)
        scaled[at, :] = jnp.zeros((chunk, cols), jnp.float32)
        squares[at, :] = jnp.zeros((chunk, LANES), jnp.float32)

        @pl.loop(0, RING)
        def _(big):
            scaled[at, :] += lax.dot_general(
                gathered[c, big], student[big], CONTRACT_LAST, preferred_element_type=jnp.float32
            )
            total = squares[at, :]
            for j in range(RING * feats // LANES):
                value = gathered[c, big, :, j * LANES:(j + 1) * LANES].astype(jnp.float32)
                total += value * value
            squares[at, :] = total

        by_block(first_rows, None, c * (chunk // ROW_BLOCK), chunk // ROW_BLOCK)

    @pl.loop(0, CHUNKS + 5)
    def _(slot):
        def due(stage):
            return (slot >= stage) & (slot < CHUNKS + stage)

        @pl.when(due(0))
        def _():
            theirs[slot] = project(slot, 1 - hid)
            core_copy(slot).start()

        @pl.when(due(1))
        def _():
            c = slot - 1
            core_copy(c).wait_recv()
            block(c, minor)[...] = (mine[lax.rem(c, 2)] + incoming[c]).astype(jnp.bfloat16)
            sends(c, 0).start()
            sends(c, 1).start()

        @pl.when(due(0))
        def _():
            mine[lax.rem(slot, 2)] = project(slot, hid)

        for stage in (2, 3, 4, 5):
            @pl.when(due(stage))
            def _():
                c = slot - stage
                near, far = 2 * stage - 4, 2 * stage - 3
                arrives(c, near).wait_recv()
                if stage in (2, 4):
                    sends(c, near + 2).start()
                arrives(c, far).wait_recv()
                if stage == 3:
                    sends(c, near + 2).start()
                if stage < 5:
                    sends(c, far + 2).start()
                else:
                    multiply(c)

        @pl.when(slot == CHUNKS - 1)
        def _():
            student_norms()

    @pl.loop(0, CHUNKS)
    def _(c):
        core_copy(c).wait_send()
        for k in range(8):
            sends(c, k).wait_send()

    def exchange(slots, own, peer, phase):
        @pl.loop(1, peers)
        def _(step):
            pltpu.make_async_remote_copy(
                src_ref=slots.at[own], dst_ref=slots.at[own],
                send_sem=send_sem.at[phase], recv_sem=recv_sem.at[phase],
                device_id=peer(step),
            ).start()

        whole = slots.at[pl.ds(0, peers - 1)]
        done = pltpu.make_async_remote_copy(
            src_ref=whole, dst_ref=whole,
            send_sem=send_sem.at[phase], recv_sem=recv_sem.at[phase],
            device_id=peer(1),
        )
        done.wait_recv()
        done.wait_send()

    row_first[stu] = jnp.concatenate(
        [to_lanes(highest[...], jnp.max), to_lanes(right[...], jnp.sum), to_lanes(spare[...], jnp.sum)],
        axis=1,
    )
    exchange(row_first, stu, stu_peer, 0)
    top, total, row_count = merge(row_first[...], rows)
    row_log = jnp.log(row_count)
    row_pot = row_log - (top + jnp.log(total))
    left[...] = to_rows(row_pot)

    def largest(at, tops):
        pot = left[at, :]
        new = []
        for strip, top in zip(strips, tops):
            value = scaled[at, strip] + pot
            scaled[at, strip] = value
            new.append(jnp.maximum(top, jnp.max(value.reshape(-1, 8, LANES), axis=0)))
        return new

    tops = by_block(largest, [jnp.full((8, LANES), SAFE, jnp.float32) for _ in strips])
    col_top = [jnp.max(top, axis=0, keepdims=True) for top in tops]

    def first_cols(at, carry):
        new = []
        for strip, top, (total, count) in zip(strips, col_top, carry):
            value = scaled[at, strip]
            term = jnp.exp(value - top)
            scaled[at, strip] = term
            total = total + jnp.sum(term.reshape(-1, 8, LANES), axis=0)
            member = jnp.where(value > SAFE, 1.0, 0.0)
            count = count + jnp.sum(member.reshape(-1, 8, LANES), axis=0)
            new.append((total, count))
        return new

    blank = jnp.zeros((8, LANES), jnp.float32)
    sums = by_block(first_cols, [(blank, blank) for _ in strips])
    total = [jnp.sum(total, axis=0, keepdims=True) for total, _ in sums]
    count = [jnp.sum(count, axis=0, keepdims=True) for _, count in sums]
    local_top = jnp.concatenate(col_top, axis=1)
    col_first[place] = jnp.concatenate(col_top + total + count, axis=1)
    exchange(col_first, place, tea_peer, 1)
    top, total, col_count = merge(col_first[...], cols)
    col_log = jnp.log(col_count)
    col_pot = col_log - (top + jnp.log(total))
    gain = jnp.exp(local_top + col_pot)
    first_pot = row_pot

    for step in range(1, ITERS):
        gains = [gain[:, strip] for strip in strips]

        def later_rows(at, carry):
            total = scaled[at, strips[0]] * gains[0]
            for strip, factor in zip(strips[1:], gains[1:]):
                total += scaled[at, strip] * factor
            right[at, :] = total
            return carry

        by_block(later_rows)
        row_next[step - 1, stu] = to_lanes(right[...], jnp.sum)
        exchange(row_next.at[step - 1], stu, stu_peer, 2 * step)
        total = jnp.sum(row_next[step - 1], axis=0)
        fresh = row_count / total
        row_pot = first_pot + jnp.log(fresh)
        left[...] = to_rows(fresh)

        def later_cols(at, sums):
            factor = left[at, :]
            return [
                total + jnp.sum((scaled[at, strip] * factor).reshape(-1, 8, LANES), axis=0)
                for strip, total in zip(strips, sums)
            ]

        sums = by_block(later_cols, [blank for _ in strips])
        total = jnp.concatenate([jnp.sum(s, axis=0, keepdims=True) for s in sums], axis=1)
        col_next[step - 1, place] = total * gain
        exchange(col_next.at[step - 1], place, tea_peer, 2 * step + 1)
        fresh = col_count / jnp.sum(col_next[step - 1], axis=0)
        col_pot = col_pot + jnp.log(fresh)
        gain = gain * fresh

    gains = [gain[:, strip] for strip in strips]

    def finish(at, carry):
        factor = left[at, :]
        for strip, other in zip(strips, gains):
            plan_ref[at, strip] = (scaled[at, strip] * factor * other).astype(jnp.bfloat16)
        return carry

    by_block(finish)
    row_out[...] = row_pot
    col_out[...] = col_pot


def per_device(peers, teacher_hidden, projection, student_hidden, teacher_segment, student_segment):
    rows, cols, feats = teacher_segment.shape[0], student_segment.shape[0], projection.shape[0]
    depth = teacher_hidden.shape[1]
    chunk = rows // CHUNKS
    vmem = pl.BlockSpec(memory_space=pltpu.VMEM)
    anywhere = pl.BlockSpec(memory_space=pl.ANY)
    plan, row_pot, col_pot = pl.pallas_call(
        functools.partial(kernel, peers),
        out_shape=(
            jax.ShapeDtypeStruct((rows, cols), jnp.bfloat16),
            jax.ShapeDtypeStruct((1, rows), jnp.float32),
            jax.ShapeDtypeStruct((1, cols), jnp.float32),
        ),
        in_specs=[anywhere] * 3 + [vmem] * 2,
        out_specs=(vmem, vmem, vmem),
        scratch_shapes=[
            pltpu.VMEM((2 * CHUNKS, chunk, depth), jnp.bfloat16),
            pltpu.VMEM((feats, depth), jnp.bfloat16),
            pltpu.VMEM((RING, cols, RING * feats), jnp.bfloat16),
            pltpu.VMEM((CHUNKS, chunk, feats), jnp.float32),
            pltpu.VMEM((2, chunk, feats), jnp.float32),
            pltpu.VMEM((CHUNKS, chunk, feats), jnp.float32),
            pltpu.VMEM((CHUNKS, RING, chunk, RING * feats), jnp.bfloat16),
            pltpu.VMEM((rows, LANES), jnp.float32),
            pltpu.VMEM((rows, LANES), jnp.float32),
            pltpu.VMEM((1, cols), jnp.float32),
            pltpu.VMEM((rows, cols), jnp.float32),
            pltpu.VMEM((rows, LANES), jnp.float32),
            pltpu.VMEM((rows, LANES), jnp.float32),
            pltpu.VMEM((rows, LANES), jnp.float32),
            pltpu.VMEM((peers, 1, 3 * rows), jnp.float32),
            pltpu.VMEM((ITERS - 1, peers, 1, rows), jnp.float32),
            pltpu.VMEM((peers, 1, 3 * cols), jnp.float32),
            pltpu.VMEM((ITERS - 1, peers, 1, cols), jnp.float32),
            pltpu.SemaphoreType.DMA((2 * CHUNKS,)),
            pltpu.SemaphoreType.DMA((2,)),
            pltpu.SemaphoreType.DMA((CHUNKS,)),
            pltpu.SemaphoreType.DMA((CHUNKS,)),
            pltpu.SemaphoreType.DMA((CHUNKS, 8)),
            pltpu.SemaphoreType.DMA((CHUNKS, 8)),
            pltpu.SemaphoreType.DMA((2 * ITERS,)),
            pltpu.SemaphoreType.DMA((2 * ITERS,)),
        ],
        compiler_params=pltpu.CompilerParams(
            collective_id=1, has_side_effects=True, vmem_limit_bytes=60 * 1024 * 1024
        ),
    )(teacher_hidden, projection, student_hidden, teacher_segment[None, :], student_segment[None, :])
    return plan, row_pot[0], col_pot[0]


def solution(mesh):
    placed = (P("tea", "hid"), P("stu", "hid"), P("stu", None), P(("tea", "hid")), P("stu"))
    return jax.shard_map(
        functools.partial(per_device, mesh.shape["stu"]),
        mesh=mesh,
        in_specs=placed,
        out_specs=(P(("tea", "hid"), "stu"), P(("tea", "hid")), P("stu")),
        check_vma=False,
    )
```

time: 534 us -> 107 us (0.20)
  blocking collectives: 363 us -> 0 us
  Pallas kernels: 0 us -> 101 us
  waiting for transfers between devices: 92.8 us -> 0 us
  other arithmetic: 39.8 us -> 1.28 us
  matrix products: 20.9 us -> 0 us
  between operations: 14.2 us -> 0.65 us
    pmax x6 -> x0, blocking collectives: 206 us -> none  [the longest x3 114 us: col_lse(): top = lax.pmax(top, ('tea', 'hid'))]
    psum x6 -> x0, blocking collectives: 157 us -> none  [the longest x3 86 us: row_lse(): total = lax.psum(shifted_sum(values, support, top, 1), 'stu')]
    pallas_call x0 -> x1, Pallas kernels: none -> 101 us  [per_device(): pl.pallas_call(functools.partial(kernel, peers), out_shape=(jax.ShapeDtyp...]
    all_gather x1 -> x0, waiting for transfers between devices: 73.5 us -> none  [per_device(): piece = lax.all_gather(projected, 'stu', axis=0, tiled=True)]
    dot_general x2 -> x0, matrix products: 20.9 us -> none  [the longest x1 11.4 us: per_device(): lax.dot_general(piece, student_hidden, CONTRACT_FIRST, preferred_element_...]
    reduce_scatter x1 -> x0, waiting for transfers between devices: 19.3 us -> none  [per_device(): lax.psum_scatter(partial_proj, 'hid', scatter_dimension=1, tiled=True)]
    reduce_sum x7 -> x0, other arithmetic: 14.4 us -> none  [the longest x6 13.9 us: shifted_sum(): return jnp.sum(terms, axis=axis)]
    reduce_max x5 -> x0, other arithmetic: 10.9 us -> none  [the longest x3 6.46 us: col_lse(): top = jnp.max(jnp.where(support, values, FLOOR), axis=0)]
  transfers between devices with their start and end apart: 2 -> 0, of which waited for: 2 -> 0; matrix products, arithmetic and copies ran while one was open for 1% -> 0% of each run, Pallas kernels for 0% -> 0%
where the time goes in v1:
time: 107 us
  Pallas kernels  101 us (94%)
  local copies, waits for them, and re-layouts  4.35 us (4%)
  other arithmetic  1.28 us (1%)
    pallas_call x1, Pallas kernels, per_device(): pl.pallas_call(functools.partial(kernel, peers), out_shape=(jax.ShapeDtyp...  101 us
    unnamed x4, local copies, waits for them, and re-layouts  3.08 us

profile of v1, /device:TPU:1, one launch (start us, length us, event | category | flops | bytes accessed | tf_op | source)
XLA Modules:
  0.0 107.1 jit_solution(11618091370113811038)
XLA Ops:
  0.6 1.3 %broadcast_in_dim.7.sseg_ref = s32[1,640]{1,0:T(1,128)} reshape(s32[640]{0:T(1024)} %param.9) | data formatting | bytes 5120 | tf_op jit(solution)/shard_map/broadcast_in_dim | solution.py:421
  1.9 100.8 %shard_map.76 = (bf16[1024,640]{1,0:T(8,128)(2,1)}, f32[1,1024]{1,0:T(1,128)}, f32[1,640]{1,0:T(1,128)}) custom-call(bf16[2048,4096]{1,0:T(8,128)(2,1)} %teacher_ref.1, bf16[256,4096]{1,0:T(8,128)(2,1)} %proj_ref.1, bf16[640,4096]{1,0:T(8,128)(2,1)} %student_ref.1, s32[1,1024]{1,0:T(1,128)} %bitcast.2, s32[1,640]{1,0:T(1,128)} %broadcast_in_dim.7.sseg_ref), custom_call_target="tpu_custom_call" | custom-call | tf_op jit(solution)/shard_map/pallas_call | solution.py:381
  102.7 0.0 copy-start
  102.7 1.3 %reduce = f32[640]{0:T(1024)} reduce(f32[1,640]{1,0:T(1,128)} %get-tuple-element.8, f32[]{:T(128)} %constant), dimensions={0}, to_apply=%get-tuple-element.8.reduce_sub_computation | reduce | bytes 5124 | tf_op jit(solution)/shard_map/pallas_call | solution.py:381
  104.0 2.5 %copy.10 = bf16[1024,640]{1,0:T(8,128)(2,1)} copy(bf16[1024,640]{1,0:T(8,128)(2,1)} %get-tuple-element.12) | data formatting | bytes 2621440
  106.5 0.0 copy-done
  106.5 0.6 copy.11
Async XLA Ops:
  102.7 3.8 %copy-start = (f32[1,1024]{1,0:T(1,128)S(1)}, f32[1,1024]{1,0:T(1,128)}, u32[]{:S(2)}) copy-start(f32[1,1024]{1,0:T(1,128)} %get-tuple-element.7) | copy-start | bytes 12292

commit v2 on v1

v2 whole, which is shorter than its diff:
```python
import functools

import jax
import jax.numpy as jnp
import numpy as np
from jax import lax
from jax.experimental import pallas as pl
from jax.experimental.pallas import tpu as pltpu
from jax.sharding import PartitionSpec as P

ITERS = 3
INV_EPSILON = float(np.float32(1.0) / np.float32(0.004))
FLOOR = -1e30
SAFE = -1e29
LANES = 128
ROW_BLOCK = 128
CHUNKS = 4
RING = 4
REACH = 2
CONTRACT_LAST = (((1,), (1,)), ((), ()))


def to_lanes(part, combine):
    return combine(jnp.transpose(part), axis=0, keepdims=True)


def to_rows(vector):
    count = vector.shape[1]
    return jnp.transpose(jnp.broadcast_to(vector, (LANES, count)))


def merge(slots, width):
    tops, sums, counts = (slots[:, :, k * width:(k + 1) * width] for k in range(3))
    top = jnp.max(tops, axis=0)
    total = jnp.sum(sums * jnp.exp(tops - top), axis=0)
    count = jnp.sum(counts, axis=0)
    return jnp.log(count) - (top + jnp.log(total)), count


def kernel(
    peers,
    teacher_ref, proj_ref, student_ref, tseg_ref, sseg_ref,
    plan_ref, row_out, col_out,
    teacher, proj, student, theirs, mine, incoming, gathered, squares, highest, sinv,
    scaled, left, right, spare, gains, row_pots, row_first, row_next, row_last, col_first, col_next, col_last,
    teacher_sem, weight_sem, core_send, core_recv, ring_send, ring_recv, near_send, near_recv, far_send, far_recv,
):
    rows, cols = scaled.shape
    feats = proj.shape[0]
    chunk = rows // CHUNKS
    half = chunk // 2
    blocks = rows // ROW_BLOCK
    strips = [slice(k * LANES, (k + 1) * LANES) for k in range(cols // LANES)]
    cores = 2
    stu = lax.axis_index("stu")
    hid = lax.axis_index("hid")
    place = lax.axis_index("tea") * cores + hid

    y, x = stu // RING, lax.rem(stu, RING)
    major, minor = y + hid * (x - y), x + hid * (y - x)

    def stu_of(big, small):
        return (big + hid * (small - big)) * RING + small + hid * (big - small)

    def around(index, step):
        return lax.rem(index + step + RING, RING)

    def stu_peer(step):
        return {"stu": lax.rem(stu + step + peers, peers)}

    def tea_peer(step):
        other = lax.rem(place + step + peers, peers)
        return {"tea": other // cores, "hid": lax.rem(other, cores)}

    def teacher_copy(c, whose):
        start = pl.multiple_of((whose * CHUNKS + c) * chunk, chunk)
        return pltpu.make_async_copy(
            teacher_ref.at[pl.ds(start, chunk)], teacher.at[whose * CHUNKS + c], teacher_sem.at[whose * CHUNKS + c]
        )

    proj_copy = pltpu.make_async_copy(proj_ref, proj, weight_sem.at[0])
    proj_copy.start()

    @pl.loop(0, CHUNKS)
    def _(c):
        teacher_copy(c, 1 - hid).start()
        teacher_copy(c, hid).start()

    @pl.loop(0, peers)
    def _(slot):
        big, small = slot // RING, lax.rem(slot, RING)
        source = pl.multiple_of(stu_of(big, small) * feats, feats)
        target = pl.multiple_of(small * feats, feats)
        pltpu.make_async_copy(
            student_ref.at[:, pl.ds(source, feats)], student.at[big, :, pl.ds(target, feats)], weight_sem.at[1]
        ).start()

    sseg = sseg_ref[...].reshape(1, cols).astype(jnp.float32)
    barrier = pltpu.get_barrier_semaphore()

    @pl.loop(1, peers)
    def _(step):
        pl.semaphore_signal(barrier, inc=1, device_id=stu_peer(step))
        pl.semaphore_signal(barrier, inc=1, device_id=tea_peer(step))

    proj_copy.wait()

    def project(c, whose):
        teacher_copy(c, whose).wait()
        return lax.dot_general(
            teacher[whose * CHUNKS + c], proj[...], CONTRACT_LAST, preferred_element_type=jnp.float32
        )

    def core_copy(c):
        return pltpu.make_async_remote_copy(
            src_ref=theirs.at[c], dst_ref=incoming.at[c],
            send_sem=core_send.at[c], recv_sem=core_recv.at[c], device_id={"hid": 1 - hid},
        )

    def ring_copy(c, stage, ref, big, small):
        return pltpu.make_async_remote_copy(
            src_ref=ref, dst_ref=ref,
            send_sem=ring_send.at[c, stage], recv_sem=ring_recv.at[c, stage],
            device_id={"stu": stu_of(around(big, 0), around(small, 0))},
        )

    def block(c, small, part=slice(None)):
        return gathered.at[c, major, part, pl.ds(pl.multiple_of(around(small, 0) * feats, feats), feats)]

    def bundle(c, big, part=slice(None)):
        return gathered.at[c, around(big, 0), part]

    low, high = pl.ds(0, half), pl.ds(half, half)

    def sends(c, k):
        return [
            lambda: ring_copy(c, 0, block(c, minor), major, minor + 1),
            lambda: ring_copy(c, 1, block(c, minor), major, minor - 1),
            lambda: ring_copy(c, 2, block(c, minor - 1, low), major, minor + 1),
            lambda: ring_copy(c, 3, block(c, minor + 1, high), major, minor - 1),
            lambda: ring_copy(c, 4, bundle(c, major), major + 1, minor),
            lambda: ring_copy(c, 5, bundle(c, major), major - 1, minor),
            lambda: ring_copy(c, 6, bundle(c, major - 1, low), major + 1, minor),
            lambda: ring_copy(c, 7, bundle(c, major + 1, high), major - 1, minor),
        ][k]()

    def arrives(c, k):
        return [
            lambda: ring_copy(c, 0, block(c, minor - 1), major, minor + 1),
            lambda: ring_copy(c, 1, block(c, minor + 1), major, minor - 1),
            lambda: ring_copy(c, 2, block(c, minor + 2, low), major, minor + 1),
            lambda: ring_copy(c, 3, block(c, minor + 2, high), major, minor - 1),
            lambda: ring_copy(c, 4, bundle(c, major - 1), major + 1, minor),
            lambda: ring_copy(c, 5, bundle(c, major + 1), major - 1, minor),
            lambda: ring_copy(c, 6, bundle(c, major + 2, low), major + 1, minor),
            lambda: ring_copy(c, 7, bundle(c, major + 2, high), major - 1, minor),
        ][k]()

    def by_block(body, init=None, first=0, count=blocks):
        def step(b, carry):
            return body(pl.ds(pl.multiple_of(b * ROW_BLOCK, ROW_BLOCK), ROW_BLOCK), carry)
        return lax.fori_loop(first, first + count, step, init)

    def student_norms():
        pltpu.make_async_copy(student, student, weight_sem.at[1]).wait()

        @pl.loop(0, cols // LANES)
        def _(k):
            at = pl.ds(pl.multiple_of(k * LANES, LANES), LANES)
            def add(big, total):
                for j in range(RING * feats // LANES):
                    value = student[big, at, j * LANES:(j + 1) * LANES].astype(jnp.float32)
                    total += value * value
                return total
            total = lax.fori_loop(0, RING, add, jnp.zeros((LANES, LANES), jnp.float32))
            sinv[:, at] = lax.rsqrt(to_lanes(total, jnp.sum) + 1e-06)

    def first_rows(at, carry):
        tinv = lax.rsqrt(jnp.sum(squares[at, :], axis=1, keepdims=True) + 1e-06)
        tseg = left[at, :]
        tops = jnp.full((ROW_BLOCK, LANES), SAFE, jnp.float32)
        count = jnp.zeros((ROW_BLOCK, LANES), jnp.float32)
        for strip in strips:
            support = tseg == sseg[:, strip]
            value = (scaled[at, strip] * tinv * sinv[:, strip] - 1.0) * INV_EPSILON
            value = jnp.where(support, value, FLOOR)
            scaled[at, strip] = value
            tops = jnp.maximum(tops, value)
            count += jnp.where(support, 1.0, 0.0)
        top = jnp.max(tops, axis=1, keepdims=True)
        total = jnp.zeros((ROW_BLOCK, LANES), jnp.float32)
        for strip in strips:
            total += jnp.exp(scaled[at, strip] - top)
        highest[at, :] = jnp.broadcast_to(top, (ROW_BLOCK, LANES))
        right[at, :] = total
        spare[at, :] = count
        return carry

    def rows_of(c):
        return pl.ds(pl.multiple_of(c * chunk, chunk), chunk)

    def product(c, big):
        return lax.dot_general(
            gathered[c, big], student[big], CONTRACT_LAST, preferred_element_type=jnp.float32
        )

    def squared(c, big, total):
        for j in range(RING * feats // LANES):
            value = gathered[c, big, :, j * LANES:(j + 1) * LANES].astype(jnp.float32)
            total += value * value
        return total

    @pl.loop(0, CHUNKS + 4)
    def _(slot):
        def due(stage):
            return (slot >= stage) & (slot < CHUNKS + stage)

        @pl.when(due(0))
        def _():
            theirs[slot] = project(slot, 1 - hid)

        @pl.when(slot == 0)
        def _():
            left[...] = to_rows(tseg_ref[...].reshape(1, rows).astype(jnp.float32))
            pl.semaphore_wait(barrier, 2 * (peers - 1))

        @pl.when(due(0))
        def _():
            core_copy(slot).start()

        @pl.when(due(1))
        def _():
            c = slot - 1
            core_copy(c).wait_recv()
            block(c, minor)[...] = (mine[lax.rem(c, 2)] + incoming[c]).astype(jnp.bfloat16)
            sends(c, 0).start()
            sends(c, 1).start()

        @pl.when(due(0))
        def _():
            mine[lax.rem(slot, 2)] = project(slot, hid)

        @pl.when(due(3))
        def _():
            c = slot - 3
            arrives(c, 0).wait_recv()
            sends(c, 2).start()
            arrives(c, 1).wait_recv()
            sends(c, 3).start()

        @pl.when(due(4))
        def _():
            c = slot - 4
            arrives(c, 2).wait_recv()
            arrives(c, 3).wait_recv()
            sends(c, 4).start()
            sends(c, 5).start()

    student_norms()

    @pl.loop(0, CHUNKS)
    def _(c):
        arrives(c, 4).wait_recv()
        sends(c, 6).start()
        arrives(c, 5).wait_recv()
        sends(c, 7).start()
        at = rows_of(c)
        before, after = around(major, -1), around(major, 1)
        scaled[at, :] = product(c, major) + product(c, before) + product(c, after)
        total = squared(c, major, jnp.zeros((chunk, LANES), jnp.float32))
        squares[at, :] = squared(c, after, squared(c, before, total))

    def near_copy(slots, peer, phase, step):
        return pltpu.make_async_remote_copy(
            src_ref=slots.at[REACH], dst_ref=slots.at[REACH - step],
            send_sem=near_send.at[phase], recv_sem=near_recv.at[phase], device_id=peer(step),
        )

    def near_start(slots, peer, phase):
        for step in (-2, -1, 1, 2):
            near_copy(slots, peer, phase, step).start()

    def near_all(slots, peer, phase):
        whole = slots.at[pl.ds(0, 2 * REACH)]
        return pltpu.make_async_remote_copy(
            src_ref=whole, dst_ref=whole,
            send_sem=near_send.at[phase], recv_sem=near_recv.at[phase], device_id=peer(1),
        )

    def spread_copy(ref, peer, phase, step):
        return pltpu.make_async_remote_copy(
            src_ref=ref, dst_ref=ref, send_sem=far_send.at[phase], recv_sem=far_recv.at[phase], device_id=peer(step)
        )

    def spread_start(slots, own, peer, phase):
        @pl.loop(1, peers)
        def _(step):
            spread_copy(slots.at[own], peer, phase, step).start()

    def spread_all(slots, peer, phase):
        return spread_copy(slots.at[pl.ds(0, peers - 1)], peer, phase, 1)

    def row_phase(step, c):
        return step * CHUNKS + c

    def col_phase(step):
        return ITERS * CHUNKS + step

    def fold(values):
        return jnp.sum(values.reshape(-1, 8, LANES), axis=0)

    def block_of(c, init, body):
        return by_block(body, init, c * (chunk // ROW_BLOCK), chunk // ROW_BLOCK)

    blank = jnp.zeros((8, LANES), jnp.float32)
    lowest = jnp.full((8, LANES), SAFE, jnp.float32)

    def complete(c):
        arrives(c, 6).wait_recv()
        arrives(c, 7).wait_recv()
        at = rows_of(c)
        opposite = around(major, 2)
        scaled[at, :] += product(c, opposite)
        squares[at, :] = squared(c, opposite, squares[at, :])
        block_of(c, None, first_rows)
        row_first[c, REACH] = jnp.concatenate(
            [
                to_lanes(highest[at, :], jnp.max),
                to_lanes(right[at, :], jnp.sum),
                to_lanes(spare[at, :], jnp.sum),
            ],
            axis=1,
        )
        near_start(row_first.at[c], stu_peer, row_phase(0, c))

    def held_rows(c):
        return row_first[c, REACH, :, 2 * chunk:] > 0.0

    def first_columns(c):
        near_all(row_first.at[c], stu_peer, row_phase(0, c)).wait_recv()
        pot, count = merge(row_first[c], chunk)
        pot = jnp.where(held_rows(c), pot, 0.0)
        row_pots[c] = jnp.concatenate([pot, count], axis=1)
        left[rows_of(c), :] = to_rows(pot)

        def largest(at, tops):
            pot = left[at, :]
            new = []
            for strip, top in zip(strips, tops):
                value = scaled[at, strip] + pot
                scaled[at, strip] = value
                new.append(jnp.maximum(top, jnp.max(value.reshape(-1, 8, LANES), axis=0)))
            return new

        tops = [jnp.max(top, axis=0, keepdims=True) for top in block_of(c, [lowest] * len(strips), largest)]

        def terms(at, carry):
            new = []
            for strip, top, (total, count) in zip(strips, tops, carry):
                value = scaled[at, strip]
                term = jnp.exp(value - top)
                scaled[at, strip] = term
                new.append((total + fold(term), count + fold(jnp.where(value > SAFE, 1.0, 0.0))))
            return new

        sums = block_of(c, [(blank, blank)] * len(strips), terms)
        flat = [jnp.sum(value, axis=0, keepdims=True) for k in range(2) for value in [pair[k] for pair in sums]]
        gains[c] = jnp.concatenate(tops + flat, axis=1)

    @pl.loop(0, CHUNKS + 1)
    def _(slot):
        @pl.when(slot < CHUNKS)
        def _():
            complete(slot)

        @pl.when(slot > 0)
        def _():
            first_columns(slot - 1)

    parts = gains[...]
    local_top = jnp.max(parts[:, :, :cols], axis=0)
    local_sum = jnp.sum(parts[:, :, cols:2 * cols] * jnp.exp(parts[:, :, :cols] - local_top), axis=0)
    own_count = jnp.sum(parts[:, :, 2 * cols:], axis=0)
    col_held = own_count > 0.0
    col_first[REACH] = jnp.concatenate([local_top, local_sum, own_count], axis=1)
    near_start(col_first, tea_peer, col_phase(0))
    near_all(col_first, tea_peer, col_phase(0)).wait_recv()
    col_pot, col_count = merge(col_first[...], cols)
    col_pot = jnp.where(col_held, col_pot, 0.0)
    for c in range(CHUNKS):
        gains[c, :, :cols] = jnp.exp(gains[c, :, :cols] + col_pot)

    def later_rows(step, c):
        def body(at, carry):
            total = scaled[at, strips[0]] * gains[c, :, strips[0]]
            for strip in strips[1:]:
                total += scaled[at, strip] * gains[c, :, strip]
            right[at, :] = total
            return carry

        block_of(c, None, body)
        row_next[step - 1, c, REACH] = to_lanes(right[rows_of(c), :], jnp.sum)
        near_start(row_next.at[step - 1, c], stu_peer, row_phase(step, c))

    def later_cols(step, c, total):
        near_all(row_next.at[step - 1, c], stu_peer, row_phase(step, c)).wait_recv()
        factor = row_pots[c, :, chunk:] / jnp.sum(row_next[step - 1, c], axis=0)
        left[rows_of(c), :] = to_rows(jnp.where(held_rows(c), factor, 0.0))

        def body(at, sums):
            factor = left[at, :]
            return [value + fold(scaled[at, strip] * factor) for strip, value in zip(strips, sums)]

        sums = block_of(c, [blank] * len(strips), body)
        own = jnp.concatenate([jnp.sum(value, axis=0, keepdims=True) for value in sums], axis=1)
        return total + own * gains[c, :, :cols]

    for step in range(1, ITERS):
        last = step == ITERS - 1

        @pl.loop(0, CHUNKS)
        def _(c):
            later_rows(step, c)

        if last:
            def flat(pick):
                return jnp.concatenate([pick(c) for c in range(CHUNKS)], axis=1)

            base = flat(lambda c: jnp.where(held_rows(c), -row_pots[c, :, :chunk], SAFE))
            total = flat(lambda c: row_next[step - 1, c, REACH])
            count = flat(lambda c: row_first[c, REACH, :, 2 * chunk:])
            row_last[stu] = jnp.concatenate([base, total, count], axis=1)
            spread_start(row_last, stu, stu_peer, 0)

        total = lax.fori_loop(
            0, CHUNKS, functools.partial(later_cols, step), jnp.zeros((1, cols), jnp.float32)
        )
        col_next[step - 1, REACH] = total
        near_start(col_next.at[step - 1], tea_peer, col_phase(step))
        if last:
            base = jnp.where(col_held, -col_pot, SAFE)
            col_last[place] = jnp.concatenate([base, total, own_count], axis=1)
            spread_start(col_last, place, tea_peer, 1)
        near_all(col_next.at[step - 1], tea_peer, col_phase(step)).wait_recv()
        fresh = jnp.where(col_held, col_count / jnp.sum(col_next[step - 1], axis=0), 1.0)
        col_pot = col_pot + jnp.log(fresh)
        for c in range(CHUNKS):
            gains[c, :, :cols] = gains[c, :, :cols] * fresh

    @pl.loop(0, CHUNKS)
    def _(c):
        def body(at, carry):
            factor = left[at, :]
            for strip in strips:
                plan_ref[at, strip] = (scaled[at, strip] * factor * gains[c, :, strip]).astype(jnp.bfloat16)
            return carry

        block_of(c, None, body)

    spread_all(row_last, stu_peer, 0).wait_recv()
    row_out[...] = merge(row_last[...], rows)[0].reshape(rows)
    spread_all(col_last, tea_peer, 1).wait_recv()
    col_out[...] = merge(col_last[...], cols)[0].reshape(cols)

    spread_all(row_last, stu_peer, 0).wait_send()
    spread_all(col_last, tea_peer, 1).wait_send()
    near_all(col_first, tea_peer, col_phase(0)).wait_send()
    for step in range(1, ITERS):
        near_all(col_next.at[step - 1], tea_peer, col_phase(step)).wait_send()

    @pl.loop(0, CHUNKS)
    def _(c):
        near_all(row_first.at[c], stu_peer, row_phase(0, c)).wait_send()
        for step in range(1, ITERS):
            near_all(row_next.at[step - 1, c], stu_peer, row_phase(step, c)).wait_send()
        core_copy(c).wait_send()
        for k in range(8):
            sends(c, k).wait_send()


def per_device(peers, teacher_hidden, projection, student_hidden, teacher_segment, student_segment):
    rows, cols, feats = teacher_segment.shape[0], student_segment.shape[0], projection.shape[0]
    depth = teacher_hidden.shape[1]
    chunk = rows // CHUNKS
    vmem = pl.BlockSpec(memory_space=pltpu.VMEM)
    anywhere = pl.BlockSpec(memory_space=pl.ANY)
    plan, row_pot, col_pot = pl.pallas_call(
        functools.partial(kernel, peers),
        out_shape=(
            pltpu.VMEM((rows, cols), jnp.bfloat16),
            pltpu.VMEM((rows,), jnp.float32),
            pltpu.VMEM((cols,), jnp.float32),
        ),
        in_specs=[anywhere] * 3 + [vmem] * 2,
        out_specs=(vmem, vmem, vmem),
        scratch_shapes=[
            pltpu.VMEM((2 * CHUNKS, chunk, depth), jnp.bfloat16),
            pltpu.VMEM((feats, depth), jnp.bfloat16),
            pltpu.VMEM((RING, cols, RING * feats), jnp.bfloat16),
            pltpu.VMEM((CHUNKS, chunk, feats), jnp.float32),
            pltpu.VMEM((2, chunk, feats), jnp.float32),
            pltpu.VMEM((CHUNKS, chunk, feats), jnp.float32),
            pltpu.VMEM((CHUNKS, RING, chunk, RING * feats), jnp.bfloat16),
            pltpu.VMEM((rows, LANES), jnp.float32),
            pltpu.VMEM((rows, LANES), jnp.float32),
            pltpu.VMEM((1, cols), jnp.float32),
            pltpu.VMEM((rows, cols), jnp.float32),
            pltpu.VMEM((rows, LANES), jnp.float32),
            pltpu.VMEM((rows, LANES), jnp.float32),
            pltpu.VMEM((rows, LANES), jnp.float32),
            pltpu.VMEM((CHUNKS, 1, 3 * cols), jnp.float32),
            pltpu.VMEM((CHUNKS, 1, 2 * chunk), jnp.float32),
            pltpu.VMEM((CHUNKS, 2 * REACH + 1, 1, 3 * chunk), jnp.float32),
            pltpu.VMEM((ITERS - 1, CHUNKS, 2 * REACH + 1, 1, chunk), jnp.float32),
            pltpu.VMEM((peers, 1, 3 * rows), jnp.float32),
            pltpu.VMEM((2 * REACH + 1, 1, 3 * cols), jnp.float32),
            pltpu.VMEM((ITERS - 1, 2 * REACH + 1, 1, cols), jnp.float32),
            pltpu.VMEM((peers, 1, 3 * cols), jnp.float32),
            pltpu.SemaphoreType.DMA((2 * CHUNKS,)),
            pltpu.SemaphoreType.DMA((2,)),
            pltpu.SemaphoreType.DMA((CHUNKS,)),
            pltpu.SemaphoreType.DMA((CHUNKS,)),
            pltpu.SemaphoreType.DMA((CHUNKS, 8)),
            pltpu.SemaphoreType.DMA((CHUNKS, 8)),
            pltpu.SemaphoreType.DMA((ITERS * (CHUNKS + 1),)),
            pltpu.SemaphoreType.DMA((ITERS * (CHUNKS + 1),)),
            pltpu.SemaphoreType.DMA((2,)),
            pltpu.SemaphoreType.DMA((2,)),
        ],
        compiler_params=pltpu.CompilerParams(
            collective_id=1, has_side_effects=True, vmem_limit_bytes=60 * 1024 * 1024
        ),
    )(teacher_hidden, projection, student_hidden, teacher_segment, student_segment)
    return plan, row_pot, col_pot


def solution(mesh):
    placed = (P("tea", "hid"), P("stu", "hid"), P("stu", None), P(("tea", "hid")), P("stu"))
    return jax.shard_map(
        functools.partial(per_device, mesh.shape["stu"]),
        mesh=mesh,
        in_specs=placed,
        out_specs=(P(("tea", "hid"), "stu"), P(("tea", "hid")), P("stu")),
        check_vma=False,
    )
```

time: 107 us -> 93.5 us (0.87)
  Pallas kernels: 101 us -> 90.5 us
  local copies, waits for them, and re-layouts: 4.35 us -> 2.25 us
  other arithmetic: 1.28 us -> 0 us
    pallas_call x1, Pallas kernels: 101 us -> 90.5 us  [per_device(): pl.pallas_call(functools.partial(kernel, peers), out_shape=(pltpu.VMEM((r...]
    pallas_call x1 -> x0, other arithmetic: 1.28 us -> none  [per_device(): pl.pallas_call(functools.partial(kernel, peers), out_shape=(jax.ShapeDtyp...]
    broadcast_in_dim x1 -> x0, local copies, waits for them, and re-layouts: 1.27 us -> none  [per_device(): student_segment[None, :]]
    unnamed x4 -> x3, local copies, waits for them, and re-layouts: 3.08 us -> 2.25 us
where the time goes in v2:
time: 93.5 us; the launch traced here: 93.3 us
  Pallas kernels  90.5 us (97%)
  local copies, waits for them, and re-layouts  2.25 us (2%)
    pallas_call x1, Pallas kernels, per_device(): pl.pallas_call(functools.partial(kernel, peers), out_shape=(pltpu.VMEM((r...  90.5 us
    unnamed x3, local copies, waits for them, and re-layouts  2.25 us

profile of v2, /device:TPU:1, one launch (start us, length us, event | category | flops | bytes accessed | tf_op | source)
XLA Modules:
  0.0 93.3 jit_solution(9236636439045632603)
XLA Ops:
  0.6 90.5 %shard_map.76 = (bf16[1024,640]{1,0:T(8,128)(2,1)S(1)}, f32[1024]{0:T(1024)S(1)}, f32[640]{0:T(1024)S(1)}) custom-call(bf16[2048,4096]{1,0:T(8,128)(2,1)} %teacher_ref.1, bf16[256,4096]{1,0:T(8,128)(2,1)} %proj_ref.1, bf16[640,4096]{1,0:T(8,128)(2,1)} %student_ref.1, s32[1024]{0:T(1024)} %tseg_ref.1, s32[640]{0:T(1024)} %sseg_ref.1), custom_call_target="tpu_custom_call" | custom-call | tf_op jit(solution)/shard_map/pallas_call | solution.py:487
  91.1 1.1 %copy.11 = bf16[1024,640]{1,0:T(8,128)(2,1)} copy(bf16[1024,640]{1,0:T(8,128)(2,1)S(1)} %get-tuple-element.3) | data formatting | bytes 2621440
  92.1 0.6 copy.12
  92.7 0.6 copy.13

commit v3 on v2

--- a/solution.py
+++ b/solution.py
@@ -287,24 +287,16 @@
             send_sem=near_send.at[phase], recv_sem=near_recv.at[phase], device_id=peer(1),
         )
 
-    def spread_copy(ref, peer, phase, step):
+    def spread_copy(ref, peer, phase, step, sends=far_send, recvs=far_recv):
         return pltpu.make_async_remote_copy(
-            src_ref=ref, dst_ref=ref, send_sem=far_send.at[phase], recv_sem=far_recv.at[phase], device_id=peer(step)
-        )
-
-    def spread_start(slots, own, peer, phase):
-        @pl.loop(1, peers)
-        def _(step):
-            spread_copy(slots.at[own], peer, phase, step).start()
-
-    def spread_all(slots, peer, phase):
-        return spread_copy(slots.at[pl.ds(0, peers - 1)], peer, phase, 1)
-
-    def row_phase(step, c):
-        return step * CHUNKS + c
+            src_ref=ref, dst_ref=ref, send_sem=sends.at[phase], recv_sem=recvs.at[phase], device_id=peer(step)
+        )
+
+    def row_phase(step):
+        return CHUNKS + step - 1
 
     def col_phase(step):
-        return ITERS * CHUNKS + step
+        return CHUNKS + ITERS - 1 + step
 
     def fold(values):
         return jnp.sum(values.reshape(-1, 8, LANES), axis=0)
@@ -331,13 +323,13 @@
             ],
             axis=1,
         )
-        near_start(row_first.at[c], stu_peer, row_phase(0, c))
+        near_start(row_first.at[c], stu_peer, c)
 
     def held_rows(c):
         return row_first[c, REACH, :, 2 * chunk:] > 0.0
 
     def first_columns(c):
-        near_all(row_first.at[c], stu_peer, row_phase(0, c)).wait_recv()
+        near_all(row_first.at[c], stu_peer, c).wait_recv()
         pot, count = merge(row_first[c], chunk)
         pot = jnp.where(held_rows(c), pot, 0.0)
         row_pots[c] = jnp.concatenate([pot, count], axis=1)
@@ -384,98 +376,136 @@
     col_held = own_count > 0.0
     col_first[REACH] = jnp.concatenate([local_top, local_sum, own_count], axis=1)
     near_start(col_first, tea_peer, col_phase(0))
+
+    @pl.loop(0, CHUNKS)
+    def _(c):
+        near_all(row_first.at[c], stu_peer, c).wait_send()
+        core_copy(c).wait_send()
+        for k in range(8):
+            sends(c, k).wait_send()
+
     near_all(col_first, tea_peer, col_phase(0)).wait_recv()
     col_pot, col_count = merge(col_first[...], cols)
     col_pot = jnp.where(col_held, col_pot, 0.0)
     for c in range(CHUNKS):
         gains[c, :, :cols] = jnp.exp(gains[c, :, :cols] + col_pot)
 
-    def later_rows(step, c):
-        def body(at, carry):
-            total = scaled[at, strips[0]] * gains[c, :, strips[0]]
+    def by_chunk_block(body, init=None):
+        def step(b, carry):
+            at = pl.ds(pl.multiple_of(b * ROW_BLOCK, ROW_BLOCK), ROW_BLOCK)
+            return body(at, gains.at[b // (chunk // ROW_BLOCK)], carry)
+        return lax.fori_loop(0, blocks, step, init)
+
+    def across(pick):
+        return jnp.concatenate([pick(c) for c in range(CHUNKS)], axis=1)
+
+    row_held = across(held_rows)
+    first_pot = across(lambda c: row_pots[c, :, :chunk])
+    row_count = across(lambda c: row_pots[c, :, chunk:])
+
+    for step in range(1, ITERS):
+        last = step == ITERS - 1
+        row_slots, col_slots = row_next.at[step - 1], col_next.at[step - 1]
+
+        def later_rows(at, gain, carry):
+            total = scaled[at, strips[0]] * gain[:, strips[0]]
             for strip in strips[1:]:
-                total += scaled[at, strip] * gains[c, :, strip]
+                total += scaled[at, strip] * gain[:, strip]
             right[at, :] = total
             return carry
 
-        block_of(c, None, body)
-        row_next[step - 1, c, REACH] = to_lanes(right[rows_of(c), :], jnp.sum)
-        near_start(row_next.at[step - 1, c], stu_peer, row_phase(step, c))
-
-    def later_cols(step, c, total):
-        near_all(row_next.at[step - 1, c], stu_peer, row_phase(step, c)).wait_recv()
-        factor = row_pots[c, :, chunk:] / jnp.sum(row_next[step - 1, c], axis=0)
-        left[rows_of(c), :] = to_rows(jnp.where(held_rows(c), factor, 0.0))
-
-        def body(at, sums):
+        by_chunk_block(later_rows)
+        row_slots[REACH] = to_lanes(right[...], jnp.sum)
+        near_start(row_slots, stu_peer, row_phase(step))
+        near_all(row_slots, stu_peer, row_phase(step)).wait_recv()
+        factor = row_count / jnp.sum(row_slots[...], axis=0)
+        left[...] = to_rows(jnp.where(row_held, factor, 0.0))
+
+        def later_cols(at, gain, sums):
             factor = left[at, :]
-            return [value + fold(scaled[at, strip] * factor) for strip, value in zip(strips, sums)]
-
-        sums = block_of(c, [blank] * len(strips), body)
-        own = jnp.concatenate([jnp.sum(value, axis=0, keepdims=True) for value in sums], axis=1)
-        return total + own * gains[c, :, :cols]
-
-    for step in range(1, ITERS):
-        last = step == ITERS - 1
-
-        @pl.loop(0, CHUNKS)
-        def _(c):
-            later_rows(step, c)
-
+            return [
+                value + fold(scaled[at, strip] * factor) * gain[:, strip] for strip, value in zip(strips, sums)
+            ]
+
+        sums = by_chunk_block(later_cols, [blank] * len(strips))
+        total = jnp.concatenate([jnp.sum(value, axis=0, keepdims=True) for value in sums], axis=1)
         if last:
-            def flat(pick):
-                return jnp.concatenate([pick(c) for c in range(CHUNKS)], axis=1)
-
-            base = flat(lambda c: jnp.where(held_rows(c), -row_pots[c, :, :chunk], SAFE))
-            total = flat(lambda c: row_next[step - 1, c, REACH])
-            count = flat(lambda c: row_first[c, REACH, :, 2 * chunk:])
-            row_last[stu] = jnp.concatenate([base, total, count], axis=1)
-            spread_start(row_last, stu, stu_peer, 0)
-
-        total = lax.fori_loop(
-            0, CHUNKS, functools.partial(later_cols, step), jnp.zeros((1, cols), jnp.float32)
-        )
-        col_next[step - 1, REACH] = total
-        near_start(col_next.at[step - 1], tea_peer, col_phase(step))
-        if last:
-            base = jnp.where(col_held, -col_pot, SAFE)
-            col_last[place] = jnp.concatenate([base, total, own_count], axis=1)
-            spread_start(col_last, place, tea_peer, 1)
-        near_all(col_next.at[step - 1], tea_peer, col_phase(step)).wait_recv()
-        fresh = jnp.where(col_held, col_count / jnp.sum(col_next[step - 1], axis=0), 1.0)
+            base = jnp.where(col_held, -col_pot - jnp.log(col_count), SAFE)
+            col_last[place] = jnp.concatenate([base, total], axis=1)
+            for k in (-2, -1, 1, 2):
+                spread_copy(col_last.at[place], tea_peer, col_phase(step), k, near_send, near_recv).start()
+
+            @pl.loop(REACH + 1, peers - REACH)
+            def _(k):
+                spread_copy(col_last.at[place], tea_peer, 1, k).start()
+
+            row_last[stu] = jnp.where(row_held, first_pot + jnp.log(factor), FLOOR)
+
+            @pl.loop(1, peers)
+            def _(k):
+                spread_copy(row_last.at[stu], stu_peer, 0, k).start()
+
+            near_cols = spread_copy(
+                col_last.at[pl.ds(0, 2 * REACH)], tea_peer, col_phase(step), 1, near_send, near_recv
+            )
+            near_cols.wait_recv()
+            for k in (-2, -1, 1, 2):
+                total += col_last[lax.rem(place + k + peers, peers), :, cols:]
+        else:
+            col_slots[REACH] = total
+            near_start(col_slots, tea_peer, col_phase(step))
+            near_all(col_slots, tea_peer, col_phase(step)).wait_recv()
+            total = jnp.sum(col_slots[...], axis=0)
+        fresh = jnp.where(col_held, col_count / total, 1.0)
         col_pot = col_pot + jnp.log(fresh)
         for c in range(CHUNKS):
             gains[c, :, :cols] = gains[c, :, :cols] * fresh
 
-    @pl.loop(0, CHUNKS)
-    def _(c):
-        def body(at, carry):
-            factor = left[at, :]
-            for strip in strips:
-                plan_ref[at, strip] = (scaled[at, strip] * factor * gains[c, :, strip]).astype(jnp.bfloat16)
-            return carry
-
-        block_of(c, None, body)
-
-    spread_all(row_last, stu_peer, 0).wait_recv()
-    row_out[...] = merge(row_last[...], rows)[0].reshape(rows)
-    spread_all(col_last, tea_peer, 1).wait_recv()
-    col_out[...] = merge(col_last[...], cols)[0].reshape(cols)
-
-    spread_all(row_last, stu_peer, 0).wait_send()
-    spread_all(col_last, tea_peer, 1).wait_send()
+    def finish(at, gain, carry):
+        factor = left[at, :]
+        for strip in strips:
+            plan_ref[at, strip] = (scaled[at, strip] * factor * gain[:, strip]).astype(jnp.bfloat16)
+        return carry
+
+    by_chunk_block(finish)
+    far_rows = spread_copy(row_last.at[pl.ds(0, peers - 1)], stu_peer, 0, 1)
+    far_cols = spread_copy(col_last.at[pl.ds(0, peers - 1 - 2 * REACH)], tea_peer, 1, 1)
+    near_cols.wait_send()
     near_all(col_first, tea_peer, col_phase(0)).wait_send()
     for step in range(1, ITERS):
+        near_all(row_next.at[step - 1], stu_peer, row_phase(step)).wait_send()
+    for step in range(1, ITERS - 1):
         near_all(col_next.at[step - 1], tea_peer, col_phase(step)).wait_send()
-
-    @pl.loop(0, CHUNKS)
-    def _(c):
-        near_all(row_first.at[c], stu_peer, row_phase(0, c)).wait_send()
-        for step in range(1, ITERS):
-            near_all(row_next.at[step - 1, c], stu_peer, row_phase(step, c)).wait_send()
-        core_copy(c).wait_send()
-        for k in range(8):
-            sends(c, k).wait_send()
+    far_rows.wait_recv()
+    row_out[...] = jnp.max(row_last[...], axis=0).reshape(rows)
+    far_cols.wait_recv()
+    base, total = col_last[:, :, :cols], col_last[:, :, cols:]
+    top = jnp.max(base, axis=0)
+    col_out[...] = -(top + jnp.log(jnp.sum(total * jnp.exp(base - top), axis=0))).reshape(cols)
+
+    far_rows.wait_send()
+    far_cols.wait_send()
+
+def hand_over_kernel(plan_ref, row_ref, col_ref, plan_out, row_out, col_out, sems):
+    copies = [
+        pltpu.make_async_copy(source, target, sems.at[k])
+        for k, (source, target) in enumerate(((plan_ref, plan_out), (row_ref, row_out), (col_ref, col_out)))
+    ]
+    for copy in copies:
+        copy.start()
+    for copy in copies:
+        copy.wait()
+
+
+def hand_over(*held):
+    anywhere = pl.BlockSpec(memory_space=pl.ANY)
+    return pl.pallas_call(
+        hand_over_kernel,
+        out_shape=tuple(jax.ShapeDtypeStruct(value.shape, value.dtype) for value in held),
+        in_specs=[pl.BlockSpec(memory_space=pltpu.VMEM)] * len(held),
+        out_specs=(anywhere,) * len(held),
+        scratch_shapes=[pltpu.SemaphoreType.DMA((len(held),))],
+    )(*(pltpu.with_memory_space_constraint(value, pltpu.VMEM) for value in held))
 
 
 def per_device(peers, teacher_hidden, projection, student_hidden, teacher_segment, student_segment):
@@ -511,19 +541,19 @@
             pltpu.VMEM((CHUNKS, 1, 3 * cols), jnp.float32),
             pltpu.VMEM((CHUNKS, 1, 2 * chunk), jnp.float32),
             pltpu.VMEM((CHUNKS, 2 * REACH + 1, 1, 3 * chunk), jnp.float32),
-            pltpu.VMEM((ITERS - 1, CHUNKS, 2 * REACH + 1, 1, chunk), jnp.float32),
-            pltpu.VMEM((peers, 1, 3 * rows), jnp.float32),
+            pltpu.VMEM((ITERS - 1, 2 * REACH + 1, 1, rows), jnp.float32),
+            pltpu.VMEM((peers, 1, rows), jnp.float32),
             pltpu.VMEM((2 * REACH + 1, 1, 3 * cols), jnp.float32),
             pltpu.VMEM((ITERS - 1, 2 * REACH + 1, 1, cols), jnp.float32),
-            pltpu.VMEM((peers, 1, 3 * cols), jnp.float32),
+            pltpu.VMEM((peers, 1, 2 * cols), jnp.float32),
             pltpu.SemaphoreType.DMA((2 * CHUNKS,)),
             pltpu.SemaphoreType.DMA((2,)),
             pltpu.SemaphoreType.DMA((CHUNKS,)),
             pltpu.SemaphoreType.DMA((CHUNKS,)),
             pltpu.SemaphoreType.DMA((CHUNKS, 8)),
             pltpu.SemaphoreType.DMA((CHUNKS, 8)),
-            pltpu.SemaphoreType.DMA((ITERS * (CHUNKS + 1),)),
-            pltpu.SemaphoreType.DMA((ITERS * (CHUNKS + 1),)),
+            pltpu.SemaphoreType.DMA((CHUNKS + 2 * ITERS - 1,)),
+            pltpu.SemaphoreType.DMA((CHUNKS + 2 * ITERS - 1,)),
             pltpu.SemaphoreType.DMA((2,)),
             pltpu.SemaphoreType.DMA((2,)),
         ],
@@ -531,7 +561,7 @@
             collective_id=1, has_side_effects=True, vmem_limit_bytes=60 * 1024 * 1024
         ),
     )(teacher_hidden, projection, student_hidden, teacher_segment, student_segment)
-    return plan, row_pot, col_pot
+    return hand_over(plan, row_pot, col_pot)
 
 
 def solution(mesh):

time: 93.5 us -> 91.8 us (0.982)
  local copies, waits for them, and re-layouts: 2.25 us -> 0 us
    unnamed x3 -> x0, local copies, waits for them, and re-layouts: 2.25 us -> none
    pallas_call x0 -> x1, Pallas kernels: none -> 1.09 us  [hand_over(): pl.pallas_call(hand_over_kernel, out_shape=tuple((jax.ShapeDtypeStruct(va...]
where the time goes in v3:
time: 91.8 us; the launch traced here: 91.6 us
  Pallas kernels  91 us (99%)
    pallas_call x1, Pallas kernels, per_device(): pl.pallas_call(functools.partial(kernel, peers), out_shape=(pltpu.VMEM((r...  89.9 us

profile of v3, /device:TPU:1, one launch (start us, length us, event | category | flops | bytes accessed | tf_op | source)
XLA Modules:
  0.0 91.6 jit_solution(2961170210465848729)
XLA Ops:
  0.6 89.9 %shard_map.76 = (bf16[1024,640]{1,0:T(8,128)(2,1)S(1)}, f32[1024]{0:T(1024)S(1)}, f32[640]{0:T(1024)S(1)}) custom-call(bf16[2048,4096]{1,0:T(8,128)(2,1)} %teacher_ref.1, bf16[256,4096]{1,0:T(8,128)(2,1)} %proj_ref.1, bf16[640,4096]{1,0:T(8,128)(2,1)} %student_ref.1, s32[1024]{0:T(1024)} %tseg_ref.1, s32[640]{0:T(1024)} %sseg_ref.1), custom_call_target="tpu_custom_call" | custom-call | tf_op jit(solution)/shard_map/pallas_call | solution.py:517
  90.5 1.1 %shard_map.77 = (bf16[1024,640]{1,0:T(8,128)(2,1)}, f32[1024]{0:T(1024)}, f32[640]{0:T(1024)}) custom-call(bf16[1024,640]{1,0:T(8,128)(2,1)S(1)} %get-tuple-element.6.plan_ref, f32[1024]{0:T(1024)S(1)} %get-tuple-element.7.row_ref, f32[640]{0:T(1024)S(1)} %get-tuple-element.8.col_ref), custom_call_target="tpu_custom_call" | custom-call | tf_op jit(solution)/shard_map/pallas_call | solution.py:502

commit v4 on v3

--- a/solution.py
+++ b/solution.py
@@ -124,37 +124,67 @@
             device_id={"stu": stu_of(around(big, 0), around(small, 0))},
         )
 
-    def block(c, small, part=slice(None)):
-        return gathered.at[c, major, part, pl.ds(pl.multiple_of(around(small, 0) * feats, feats), feats)]
+    def block(c, big, small, part=slice(None)):
+        return gathered.at[c, around(big, 0), part, pl.ds(pl.multiple_of(around(small, 0) * feats, feats), feats)]
 
     def bundle(c, big, part=slice(None)):
         return gathered.at[c, around(big, 0), part]
 
     low, high = pl.ds(0, half), pl.ds(half, half)
-
-    def sends(c, k):
-        return [
-            lambda: ring_copy(c, 0, block(c, minor), major, minor + 1),
-            lambda: ring_copy(c, 1, block(c, minor), major, minor - 1),
-            lambda: ring_copy(c, 2, block(c, minor - 1, low), major, minor + 1),
-            lambda: ring_copy(c, 3, block(c, minor + 1, high), major, minor - 1),
-            lambda: ring_copy(c, 4, bundle(c, major), major + 1, minor),
-            lambda: ring_copy(c, 5, bundle(c, major), major - 1, minor),
-            lambda: ring_copy(c, 6, bundle(c, major - 1, low), major + 1, minor),
-            lambda: ring_copy(c, 7, bundle(c, major + 1, high), major - 1, minor),
-        ][k]()
-
-    def arrives(c, k):
-        return [
-            lambda: ring_copy(c, 0, block(c, minor - 1), major, minor + 1),
-            lambda: ring_copy(c, 1, block(c, minor + 1), major, minor - 1),
-            lambda: ring_copy(c, 2, block(c, minor + 2, low), major, minor + 1),
-            lambda: ring_copy(c, 3, block(c, minor + 2, high), major, minor - 1),
-            lambda: ring_copy(c, 4, bundle(c, major - 1), major + 1, minor),
-            lambda: ring_copy(c, 5, bundle(c, major + 1), major - 1, minor),
-            lambda: ring_copy(c, 6, bundle(c, major + 2, low), major + 1, minor),
-            lambda: ring_copy(c, 7, bundle(c, major + 2, high), major - 1, minor),
-        ][k]()
+    offsets = (0, -1, 1, 2)
+
+    def along_minor(c, k, side, small, part=slice(None)):
+        return ring_copy(c, k, block(c, major, small, part), major, minor + side)
+
+    def along_major(c, which, side, big):
+        return ring_copy(
+            c, 4 + 2 * which + (side < 0), block(c, big, minor + offsets[which]), major + side, minor
+        )
+
+    def relay(c, side, big):
+        return ring_copy(c, 12 + (side < 0), bundle(c, big, low if side > 0 else high), major + side, minor)
+
+    def send_major(c, which):
+        along_major(c, which, 1, major).start()
+        along_major(c, which, -1, major).start()
+
+    def own_stage(c):
+        along_minor(c, 0, 1, minor).start()
+        along_minor(c, 1, -1, minor).start()
+        send_major(c, 0)
+
+    def near_stage(c):
+        along_minor(c, 0, 1, minor - 1).wait_recv()
+        along_minor(c, 2, 1, minor - 1, low).start()
+        send_major(c, 1)
+        along_minor(c, 1, -1, minor + 1).wait_recv()
+        along_minor(c, 3, -1, minor + 1, high).start()
+        send_major(c, 2)
+
+    def far_stage(c):
+        along_minor(c, 2, 1, minor + 2, low).wait_recv()
+        along_minor(c, 3, -1, minor + 2, high).wait_recv()
+        send_major(c, 3)
+
+    def relay_stage(c):
+        for side in (1, -1):
+            for which in range(4):
+                along_major(c, which, side, major - side).wait_recv()
+            relay(c, side, major - side).start()
+
+    def last_stage(c):
+        relay(c, 1, major + 2).wait_recv()
+        relay(c, -1, major + 2).wait_recv()
+
+    def sent(c):
+        along_minor(c, 0, 1, minor).wait_send()
+        along_minor(c, 1, -1, minor).wait_send()
+        along_minor(c, 2, 1, minor - 1, low).wait_send()
+        along_minor(c, 3, -1, minor + 1, high).wait_send()
+        for side in (1, -1):
+            for which in range(4):
+                along_major(c, which, side, major).wait_send()
+            relay(c, side, major - side).wait_send()
 
     def by_block(body, init=None, first=0, count=blocks):
         def step(b, carry):
@@ -232,9 +262,8 @@
         def _():
             c = slot - 1
             core_copy(c).wait_recv()
-            block(c, minor)[...] = (mine[lax.rem(c, 2)] + incoming[c]).astype(jnp.bfloat16)
-            sends(c, 0).start()
-            sends(c, 1).start()
+            block(c, major, minor)[...] = (mine[lax.rem(c, 2)] + incoming[c]).astype(jnp.bfloat16)
+            own_stage(c)
 
         @pl.when(due(0))
         def _():
@@ -242,28 +271,17 @@
 
         @pl.when(due(3))
         def _():
-            c = slot - 3
-            arrives(c, 0).wait_recv()
-            sends(c, 2).start()
-            arrives(c, 1).wait_recv()
-            sends(c, 3).start()
+            near_stage(slot - 3)
 
         @pl.when(due(4))
         def _():
-            c = slot - 4
-            arrives(c, 2).wait_recv()
-            arrives(c, 3).wait_recv()
-            sends(c, 4).start()
-            sends(c, 5).start()
+            far_stage(slot - 4)
 
     student_norms()
 
     @pl.loop(0, CHUNKS)
     def _(c):
-        arrives(c, 4).wait_recv()
-        sends(c, 6).start()
-        arrives(c, 5).wait_recv()
-        sends(c, 7).start()
+        relay_stage(c)
         at = rows_of(c)
         before, after = around(major, -1), around(major, 1)
         scaled[at, :] = product(c, major) + product(c, before) + product(c, after)
@@ -308,8 +326,7 @@
     lowest = jnp.full((8, LANES), SAFE, jnp.float32)
 
     def complete(c):
-        arrives(c, 6).wait_recv()
-        arrives(c, 7).wait_recv()
+        last_stage(c)
         at = rows_of(c)
         opposite = around(major, 2)
         scaled[at, :] += product(c, opposite)
@@ -381,8 +398,7 @@
     def _(c):
         near_all(row_first.at[c], stu_peer, c).wait_send()
         core_copy(c).wait_send()
-        for k in range(8):
-            sends(c, k).wait_send()
+        sent(c)
 
     near_all(col_first, tea_peer, col_phase(0)).wait_recv()
     col_pot, col_count = merge(col_first[...], cols)
@@ -550,8 +566,8 @@
             pltpu.SemaphoreType.DMA((2,)),
             pltpu.SemaphoreType.DMA((CHUNKS,)),
             pltpu.SemaphoreType.DMA((CHUNKS,)),
-            pltpu.SemaphoreType.DMA((CHUNKS, 8)),
-            pltpu.SemaphoreType.DMA((CHUNKS, 8)),
+            pltpu.SemaphoreType.DMA((CHUNKS, 14)),
+            pltpu.SemaphoreType.DMA((CHUNKS, 14)),
             pltpu.SemaphoreType.DMA((CHUNKS + 2 * ITERS - 1,)),
             pltpu.SemaphoreType.DMA((CHUNKS + 2 * ITERS - 1,)),
             pltpu.SemaphoreType.DMA((2,)),

time: 91.8 us -> 90.7 us (0.988)
  Pallas kernels: 91 us -> 89.9 us
    pallas_call x1, Pallas kernels: 89.9 us -> 88.8 us  [per_device(): pl.pallas_call(functools.partial(kernel, peers), out_shape=(pltpu.VMEM((r...]
where the time goes in v4:
time: 90.7 us; the launch traced here: 90.6 us
  Pallas kernels  89.9 us (99%)
    pallas_call x1, Pallas kernels, per_device(): pl.pallas_call(functools.partial(kernel, peers), out_shape=(pltpu.VMEM((r...  88.8 us

profile of v4, /device:TPU:1, one launch (start us, length us, event | category | flops | bytes accessed | tf_op | source)
XLA Modules:
  0.0 90.6 jit_solution(18375288552630270712)
XLA Ops:
  0.6 88.8 %shard_map.76 = (bf16[1024,640]{1,0:T(8,128)(2,1)S(1)}, f32[1024]{0:T(1024)S(1)}, f32[640]{0:T(1024)S(1)}) custom-call(bf16[2048,4096]{1,0:T(8,128)(2,1)} %teacher_ref.1, bf16[256,4096]{1,0:T(8,128)(2,1)} %proj_ref.1, bf16[640,4096]{1,0:T(8,128)(2,1)} %student_ref.1, s32[1024]{0:T(1024)} %tseg_ref.1, s32[640]{0:T(1024)} %sseg_ref.1), custom_call_target="tpu_custom_call" | custom-call | tf_op jit(solution)/shard_map/pallas_call | solution.py:533
  89.5 1.1 %shard_map.77 = (bf16[1024,640]{1,0:T(8,128)(2,1)}, f32[1024]{0:T(1024)}, f32[640]{0:T(1024)}) custom-call(bf16[1024,640]{1,0:T(8,128)(2,1)S(1)} %get-tuple-element.6.plan_ref, f32[1024]{0:T(1024)S(1)} %get-tuple-element.7.row_ref, f32[640]{0:T(1024)S(1)} %get-tuple-element.8.col_ref), custom_call_target="tpu_custom_call" | custom-call | tf_op jit(solution)/shard_map/pallas_call | solution.py:518

commit v5 on v4

--- a/solution.py
+++ b/solution.py
@@ -16,6 +16,7 @@
 ROW_BLOCK = 128
 CHUNKS = 4
 RING = 4
+TEA_HALF = 4
 REACH = 2
 CONTRACT_LAST = (((1,), (1,)), ((), ()))
 
@@ -43,7 +44,7 @@
     plan_ref, row_out, col_out,
     teacher, proj, student, theirs, mine, incoming, gathered, squares, highest, sinv,
     scaled, left, right, spare, gains, row_pots, row_first, row_next, row_last, col_first, col_next, col_last,
-    teacher_sem, weight_sem, core_send, core_recv, ring_send, ring_recv, near_send, near_recv, far_send, far_recv,
+    teacher_sem, weight_sem, core_send, core_recv, ring_send, ring_recv, near_send, near_recv, far_send, far_recv, token,
 ):
     rows, cols = scaled.shape
     feats = proj.shape[0]
@@ -72,6 +73,14 @@
         other = lax.rem(place + step + peers, peers)
         return {"tea": other // cores, "hid": lax.rem(other, cores)}
 
+    def beside(side):
+        other = lax.rem(place + 2 * side + peers, peers) // cores
+        return {"tea": other, "hid": 1 - hid}
+
+    def pass_token(k):
+        for side in (1, -1):
+            pl.semaphore_signal(token.at[k], inc=1, device_id=tea_peer(2 * side))
+
     def teacher_copy(c, whose):
         start = pl.multiple_of((whose * CHUNKS + c) * chunk, chunk)
         return pltpu.make_async_copy(
@@ -98,10 +107,12 @@
     sseg = sseg_ref[...].reshape(1, cols).astype(jnp.float32)
     barrier = pltpu.get_barrier_semaphore()
 
-    @pl.loop(1, peers)
-    def _(step):
-        pl.semaphore_signal(barrier, inc=1, device_id=stu_peer(step))
-        pl.semaphore_signal(barrier, inc=1, device_id=tea_peer(step))
+    for side in (1, -1):
+        pl.semaphore_signal(barrier, inc=1, device_id={"stu": stu_of(major, around(minor, side))})
+        pl.semaphore_signal(barrier, inc=1, device_id={"stu": stu_of(around(major, side), minor)})
+        pl.semaphore_signal(barrier, inc=1, device_id=tea_peer(2 * side))
+        pl.semaphore_signal(barrier, inc=1, device_id=beside(side))
+    pl.semaphore_signal(barrier, inc=1, device_id={"hid": 1 - hid})
 
     proj_copy.wait()
 
@@ -252,7 +263,8 @@
         @pl.when(slot == 0)
         def _():
             left[...] = to_rows(tseg_ref[...].reshape(1, rows).astype(jnp.float32))
-            pl.semaphore_wait(barrier, 2 * (peers - 1))
+            pl.semaphore_wait(barrier, 9)
+            pass_token(0)
 
         @pl.when(due(0))
         def _():
@@ -278,6 +290,10 @@
             far_stage(slot - 4)
 
     student_norms()
+    for k in range(1, TEA_HALF):
+        pl.semaphore_wait(token.at[k - 1], 2)
+        if k < TEA_HALF - 1:
+            pass_token(k)
 
     @pl.loop(0, CHUNKS)
     def _(c):
@@ -572,6 +588,7 @@
             pltpu.SemaphoreType.DMA((CHUNKS + 2 * ITERS - 1,)),
             pltpu.SemaphoreType.DMA((2,)),
             pltpu.SemaphoreType.DMA((2,)),
+            pltpu.SemaphoreType.REGULAR((TEA_HALF - 1,)),
         ],
         compiler_params=pltpu.CompilerParams(
             collective_id=1, has_side_effects=True, vmem_limit_bytes=60 * 1024 * 1024

time: 90.7 us -> 89.9 us (level)
  no operation moved by 1% of the time
where the time goes in v5:
time: 89.9 us; the launch traced here: 89.8 us
  Pallas kernels  89.1 us (99%)
    pallas_call x1, Pallas kernels, per_device(): pl.pallas_call(functools.partial(kernel, peers), out_shape=(pltpu.VMEM((r...  88 us

profile of v5, /device:TPU:1, one launch (start us, length us, event | category | flops | bytes accessed | tf_op | source)
XLA Modules:
  0.0 89.8 jit_solution(6997670187525336643)
XLA Ops:
  0.6 88.0 %shard_map.76 = (bf16[1024,640]{1,0:T(8,128)(2,1)S(1)}, f32[1024]{0:T(1024)S(1)}, f32[640]{0:T(1024)S(1)}) custom-call(bf16[2048,4096]{1,0:T(8,128)(2,1)} %teacher_ref.1, bf16[256,4096]{1,0:T(8,128)(2,1)} %proj_ref.1, bf16[640,4096]{1,0:T(8,128)(2,1)} %student_ref.1, s32[1024]{0:T(1024)} %tseg_ref.1, s32[640]{0:T(1024)} %sseg_ref.1), custom_call_target="tpu_custom_call" | custom-call | tf_op jit(solution)/shard_map/pallas_call | solution.py:549
  88.7 1.1 %shard_map.77 = (bf16[1024,640]{1,0:T(8,128)(2,1)}, f32[1024]{0:T(1024)}, f32[640]{0:T(1024)}) custom-call(bf16[1024,640]{1,0:T(8,128)(2,1)S(1)} %get-tuple-element.6.plan_ref, f32[1024]{0:T(1024)S(1)} %get-tuple-element.7.row_ref, f32[640]{0:T(1024)S(1)} %get-tuple-element.8.col_ref), custom_call_target="tpu_custom_call" | custom-call | tf_op jit(solution)/shard_map/pallas_call | solution.py:534

commit v6 on v5

--- a/solution.py
+++ b/solution.py
@@ -220,20 +220,25 @@
         tinv = lax.rsqrt(jnp.sum(squares[at, :], axis=1, keepdims=True) + 1e-06)
         tseg = left[at, :]
         tops = jnp.full((ROW_BLOCK, LANES), SAFE, jnp.float32)
-        count = jnp.zeros((ROW_BLOCK, LANES), jnp.float32)
         for strip in strips:
             support = tseg == sseg[:, strip]
             value = (scaled[at, strip] * tinv * sinv[:, strip] - 1.0) * INV_EPSILON
             value = jnp.where(support, value, FLOOR)
             scaled[at, strip] = value
             tops = jnp.maximum(tops, value)
-            count += jnp.where(support, 1.0, 0.0)
         top = jnp.max(tops, axis=1, keepdims=True)
         total = jnp.zeros((ROW_BLOCK, LANES), jnp.float32)
         for strip in strips:
             total += jnp.exp(scaled[at, strip] - top)
         highest[at, :] = jnp.broadcast_to(top, (ROW_BLOCK, LANES))
         right[at, :] = total
+        return carry
+
+    def count_rows(at, carry):
+        tseg = left[at, :]
+        count = jnp.zeros((ROW_BLOCK, LANES), jnp.float32)
+        for strip in strips:
+            count += jnp.where(tseg == sseg[:, strip], 1.0, 0.0)
         spare[at, :] = count
         return carry
 
@@ -303,6 +308,8 @@
         scaled[at, :] = product(c, major) + product(c, before) + product(c, after)
         total = squared(c, major, jnp.zeros((chunk, LANES), jnp.float32))
         squares[at, :] = squared(c, after, squared(c, before, total))
+        by_block(count_rows, None, c * (chunk // ROW_BLOCK), chunk // ROW_BLOCK)
+        row_first[c, REACH, :, 2 * chunk:] = to_lanes(spare[at, :], jnp.sum)
 
     def near_copy(slots, peer, phase, step):
         return pltpu.make_async_remote_copy(
@@ -311,7 +318,7 @@
         )
 
     def near_start(slots, peer, phase):
-        for step in (-2, -1, 1, 2):
+        for step in (-2, 2, -1, 1):
             near_copy(slots, peer, phase, step).start()
 
     def near_all(slots, peer, phase):
@@ -352,7 +359,7 @@
             [
                 to_lanes(highest[at, :], jnp.max),
                 to_lanes(right[at, :], jnp.sum),
-                to_lanes(spare[at, :], jnp.sum),
+                row_first[c, REACH, :, 2 * chunk:],
             ],
             axis=1,
         )
@@ -464,7 +471,7 @@
         if last:
             base = jnp.where(col_held, -col_pot - jnp.log(col_count), SAFE)
             col_last[place] = jnp.concatenate([base, total], axis=1)
-            for k in (-2, -1, 1, 2):
+            for k in (-2, 2, -1, 1):
                 spread_copy(col_last.at[place], tea_peer, col_phase(step), k, near_send, near_recv).start()
 
             @pl.loop(REACH + 1, peers - REACH)

time: 89.9 us -> 89.8 us (level)
  no operation moved by 1% of the time
where the time goes in v6:
time: 89.8 us; the launch traced here: 89.7 us
  Pallas kernels  89.1 us (99%)
    pallas_call x1, Pallas kernels, per_device(): pl.pallas_call(functools.partial(kernel, peers), out_shape=(pltpu.VMEM((r...  88 us

profile of v6, /device:TPU:1, one launch (start us, length us, event | category | flops | bytes accessed | tf_op | source)
XLA Modules:
  0.0 89.7 jit_solution(14902057803544651890)
XLA Ops:
  0.6 88.0 %shard_map.76 = (bf16[1024,640]{1,0:T(8,128)(2,1)S(1)}, f32[1024]{0:T(1024)S(1)}, f32[640]{0:T(1024)S(1)}) custom-call(bf16[2048,4096]{1,0:T(8,128)(2,1)} %teacher_ref.1, bf16[256,4096]{1,0:T(8,128)(2,1)} %proj_ref.1, bf16[640,4096]{1,0:T(8,128)(2,1)} %student_ref.1, s32[1024]{0:T(1024)} %tseg_ref.1, s32[640]{0:T(1024)} %sseg_ref.1), custom_call_target="tpu_custom_call" | custom-call | tf_op jit(solution)/shard_map/pallas_call | solution.py:556
  88.6 1.1 %shard_map.77 = (bf16[1024,640]{1,0:T(8,128)(2,1)}, f32[1024]{0:T(1024)}, f32[640]{0:T(1024)}) custom-call(bf16[1024,640]{1,0:T(8,128)(2,1)S(1)} %get-tuple-element.6.plan_ref, f32[1024]{0:T(1024)S(1)} %get-tuple-element.7.row_ref, f32[640]{0:T(1024)S(1)} %get-tuple-element.8.col_ref), custom_call_target="tpu_custom_call" | custom-call | tf_op jit(solution)/shard_map/pallas_call | solution.py:541

commit v7 on v6

--- a/solution.py
+++ b/solution.py
@@ -267,7 +267,6 @@
 
         @pl.when(slot == 0)
         def _():
-            left[...] = to_rows(tseg_ref[...].reshape(1, rows).astype(jnp.float32))
             pl.semaphore_wait(barrier, 9)
             pass_token(0)
 
@@ -294,6 +293,7 @@
         def _():
             far_stage(slot - 4)
 
+    left[...] = to_rows(tseg_ref[...].reshape(1, rows).astype(jnp.float32))
     student_norms()
     for k in range(1, TEA_HALF):
         pl.semaphore_wait(token.at[k - 1], 2)
@@ -380,16 +380,16 @@
             new = []
             for strip, top in zip(strips, tops):
                 value = scaled[at, strip] + pot
-                scaled[at, strip] = value
                 new.append(jnp.maximum(top, jnp.max(value.reshape(-1, 8, LANES), axis=0)))
             return new
 
         tops = [jnp.max(top, axis=0, keepdims=True) for top in block_of(c, [lowest] * len(strips), largest)]
 
         def terms(at, carry):
+            pot = left[at, :]
             new = []
             for strip, top, (total, count) in zip(strips, tops, carry):
-                value = scaled[at, strip]
+                value = scaled[at, strip] + pot
                 term = jnp.exp(value - top)
                 scaled[at, strip] = term
                 new.append((total + fold(term), count + fold(jnp.where(value > SAFE, 1.0, 0.0))))

time: 89.8 us -> 89.7 us (level)
  no operation moved by 1% of the time
where the time goes in v7:
time: 89.7 us; the launch traced here: 89.6 us
  Pallas kernels  89 us (99%)
    pallas_call x1, Pallas kernels, per_device(): pl.pallas_call(functools.partial(kernel, peers), out_shape=(pltpu.VMEM((r...  87.9 us

profile of v7, /device:TPU:1, one launch (start us, length us, event | category | flops | bytes accessed | tf_op | source)
XLA Modules:
  0.0 89.6 jit_solution(7229174128001510287)
XLA Ops:
  0.6 87.9 %shard_map.76 = (bf16[1024,640]{1,0:T(8,128)(2,1)S(1)}, f32[1024]{0:T(1024)S(1)}, f32[640]{0:T(1024)S(1)}) custom-call(bf16[2048,4096]{1,0:T(8,128)(2,1)} %teacher_ref.1, bf16[256,4096]{1,0:T(8,128)(2,1)} %proj_ref.1, bf16[640,4096]{1,0:T(8,128)(2,1)} %student_ref.1, s32[1024]{0:T(1024)} %tseg_ref.1, s32[640]{0:T(1024)} %sseg_ref.1), custom_call_target="tpu_custom_call" | custom-call | tf_op jit(solution)/shard_map/pallas_call | solution.py:556
  88.5 1.1 %shard_map.77 = (bf16[1024,640]{1,0:T(8,128)(2,1)}, f32[1024]{0:T(1024)}, f32[640]{0:T(1024)}) custom-call(bf16[1024,640]{1,0:T(8,128)(2,1)S(1)} %get-tuple-element.6.plan_ref, f32[1024]{0:T(1024)S(1)} %get-tuple-element.7.row_ref, f32[640]{0:T(1024)S(1)} %get-tuple-element.8.col_ref), custom_call_target="tpu_custom_call" | custom-call | tf_op jit(solution)/shard_map/pallas_call | solution.py:541

commit v8 on v6

--- a/solution.py
+++ b/solution.py
@@ -474,9 +474,12 @@
             for k in (-2, 2, -1, 1):
                 spread_copy(col_last.at[place], tea_peer, col_phase(step), k, near_send, near_recv).start()
 
-            @pl.loop(REACH + 1, peers - REACH)
+            others = peers - 1 - 2 * REACH
+
+            @pl.loop(0, others)
             def _(k):
-                spread_copy(col_last.at[place], tea_peer, 1, k).start()
+                step_away = REACH + 1 + lax.rem(k + others // 2, others)
+                spread_copy(col_last.at[place], tea_peer, 1, step_away).start()
 
             row_last[stu] = jnp.where(row_held, first_pot + jnp.log(factor), FLOOR)
 

time: 89.8 us -> 89.6 us (level)
  no operation moved by 1% of the time
where the time goes in v8:
time: 89.6 us; the launch traced here: 89.4 us
  Pallas kernels  88.8 us (99%)
    pallas_call x1, Pallas kernels, per_device(): pl.pallas_call(functools.partial(kernel, peers), out_shape=(pltpu.VMEM((r...  87.7 us

profile of v8, /device:TPU:1, one launch (start us, length us, event | category | flops | bytes accessed | tf_op | source)
XLA Modules:
  0.0 89.4 jit_solution(13370947754829257980)
XLA Ops:
  0.6 87.7 %shard_map.76 = (bf16[1024,640]{1,0:T(8,128)(2,1)S(1)}, f32[1024]{0:T(1024)S(1)}, f32[640]{0:T(1024)S(1)}) custom-call(bf16[2048,4096]{1,0:T(8,128)(2,1)} %teacher_ref.1, bf16[256,4096]{1,0:T(8,128)(2,1)} %proj_ref.1, bf16[640,4096]{1,0:T(8,128)(2,1)} %student_ref.1, s32[1024]{0:T(1024)} %tseg_ref.1, s32[640]{0:T(1024)} %sseg_ref.1), custom_call_target="tpu_custom_call" | custom-call | tf_op jit(solution)/shard_map/pallas_call | solution.py:559
  88.3 1.1 %shard_map.77 = (bf16[1024,640]{1,0:T(8,128)(2,1)}, f32[1024]{0:T(1024)}, f32[640]{0:T(1024)}) custom-call(bf16[1024,640]{1,0:T(8,128)(2,1)S(1)} %get-tuple-element.6.plan_ref, f32[1024]{0:T(1024)S(1)} %get-tuple-element.7.row_ref, f32[640]{0:T(1024)S(1)} %get-tuple-element.8.col_ref), custom_call_target="tpu_custom_call" | custom-call | tf_op jit(solution)/shard_map/pallas_call | solution.py:544
